TPU v7x, 256 devices: a whole 4x4x8 slice. The times are simulated.
256 devices in a mesh: row: 16 (over z, y_lo), col: 8 (over x, core), rep: 2 (over y_hi).
Axes of the slice: x: 4, y: 4 (y_hi: 2, y_lo: 2; y = y_hi * 2 + y_lo), z: 8, core: 2. Of those that a mesh axis runs over, the one named last changes fastest.
Arguments:
- a_blocks: bfloat16 [128, 16, 2, 128, 128], P('row', 'col'), may hold values from -0.25 to 0.25
- a_index: int32 [128, 16, 2], P('row', 'col'), may hold values from 0 to 63, as said below
- a_count: int32 [128, 16], P('row', 'col'), may hold values from 0 to 2, as said below
- b_blocks: bfloat16 [16, 8, 32, 128, 128], P('row', 'col'), may hold values from -6 to 6
- b_rows: int32 [16, 8, 32], P('row', 'col'), may hold values from 0 to 63, as said below
- b_cols: int32 [16, 8, 32], P('row', 'col'), may hold values from 0 to 63
- b_count: int32 [16, 8], P('row', 'col'), may hold values from 16 to 32, as said below
- c_cols: int32 [128, 8, 4], P('row', 'col'), may hold values from 0 to 63, as said below
- c_count: int32 [128, 8], P('row', 'col'), may hold values from 1 to 4, as said below
Outputs:
- c_blocks: bfloat16 [128, 8, 4, 128, 128], P(('row', 'rep'), 'col')
Inputs may be any that keep to these rules, and one draw needn't show every extreme that they name: Live slots come first: slot a of block row i in piece p is live when a < a_count[i, p]. `a_index`: the slots of one block row and piece name distinct block rows of that piece. Live slots come first: slot m of list (p, q) is live when m < b_count[p, q]. `b_rows`: the slots of one list name distinct block rows of the piece. Live slots come first: slot s of block row i in group q is live when s < c_count[i, q]. `c_cols`: the slots of one block row and group name distinct block columns.
All inputs are finite; a program needn't handle non-finite values.
Results may differ from a plain program's by a relative error of at most 0.001.
Values may be sent and summed in bfloat16 or wider, within the bound.
No kernel may reach another device: no remote copies, remote signals or barrier semaphores. Data moves between devices by JAX's collectives and lax.ppermute only.
A program may use at most 64 MiB of HBM per device.

v0:
```python
import jax
import jax.numpy as jnp
from jax import lax
from jax.sharding import PartitionSpec as P


def shortened(shard):
    return jax.tree.map(lambda a: a.astype(jnp.bfloat16) if a.dtype == jnp.float32 else a, shard)


def from_behind(value, axis, steps):
    count = lax.axis_size(axis)
    pairs = [(source, (source + steps) % count) for source in range(count)]
    return lax.ppermute(value, axis, pairs)


def accumulate(running, a_part, b_part, c_cols_loc, c_count_loc):
    a_blk, a_idx, a_cnt = a_part
    b_blk, b_row, b_col, b_cnt = b_part
    slots_a = jnp.arange(a_idx.shape[1], dtype=jnp.int32)
    slots_b = jnp.arange(b_row.shape[0], dtype=jnp.int32)
    slots_c = jnp.arange(c_cols_loc.shape[1], dtype=jnp.int32)
    a_live = slots_a[None, :] < a_cnt[:, None]
    b_live = slots_b < b_cnt[0]
    matches = (
        (a_idx[:, :, None] == b_row[None, None, :]) & b_live[None, None, :] & a_live[:, :, None]
    )
    where_b = jnp.sum(jnp.where(matches, slots_b, jnp.int32(0)), axis=-1)
    found_position = jnp.any(matches, axis=-1)
    picked = jnp.take(b_blk, where_b, axis=0)
    target = jnp.take(b_col, where_b, axis=0)
    c_live = slots_c[None, :] < c_count_loc[:, None]
    landing = (
        (c_cols_loc[:, None, :] == target[:, :, None])
        & found_position[:, :, None]
        & c_live[:, None, :]
    )
    products = jnp.einsum("iaxy,iayz->iaxz", a_blk, picked, preferred_element_type=jnp.float32)
    return running + jnp.einsum(
        "ias,iaxz->isxz", landing.astype(jnp.float32), products, precision=lax.Precision.HIGHEST
    )


def slab_take(slabs, slab_no):
    return tuple((lax.dynamic_index_in_dim(member, slab_no, 1, keepdims=False) for member in slabs))


def slab_put(slabs, a_part, slab_no):
    return tuple(
        (
            lax.dynamic_update_index_in_dim(member, update, slab_no, 1)
            for member, update in zip(slabs, a_part)
        )
    )


def align_rows(b_piece, amount, low_level, high_level):
    for exponent in range(low_level, high_level):
        arrived = jax.tree.map(
            lambda part, own: part.astype(own.dtype),
            from_behind(shortened(b_piece), "row", -(1 << exponent)),
            b_piece,
        )
        chosen = jnp.right_shift(amount, exponent) & 1 == 1
        b_piece = tuple(
            (jnp.where(chosen, shifted, before) for shifted, before in zip(arrived, b_piece))
        )
    return b_piece


def align_cols(slabs, block_totals, levels):
    for exponent in range(levels):
        arrived = jax.tree.map(
            lambda part, own: part.astype(own.dtype),
            from_behind(shortened(slabs), "col", -(1 << exponent)),
            slabs,
        )
        chosen = jnp.right_shift(block_totals, exponent) & 1 == 1
        slabs = tuple(
            (
                jnp.where(chosen.reshape((1, -1) + (1,) * (before.ndim - 2)), shifted, before)
                for shifted, before in zip(arrived, slabs)
            )
        )
    return slabs


def walk(
    slabs, b_piece, first_slab, count_of_iterations, a_hop, b_hop, c_cols_loc, c_count_loc, running
):
    slab_count = slabs[0].shape[1]

    def advance(step_no, state_tuple):
        running, slabs, b_piece = state_tuple
        slab_no = (first_slab + step_no) % slab_count
        a_part = slab_take(slabs, slab_no)
        running = accumulate(running, a_part, b_piece, c_cols_loc, c_count_loc)
        arrived = jax.tree.map(
            lambda part, own: part.astype(own.dtype),
            from_behind(shortened(a_part), "col", -a_hop),
            a_part,
        )
        slabs = slab_put(slabs, arrived, slab_no)
        b_piece = jax.tree.map(
            lambda part, own: part.astype(own.dtype),
            from_behind(shortened(b_piece), "row", -b_hop),
            b_piece,
        )
        return (running, slabs, b_piece)

    running, slabs, b_piece = lax.fori_loop(
        0, count_of_iterations - 1, advance, (running, slabs, b_piece)
    )
    final_slab = (first_slab + count_of_iterations - 1) % slab_count
    return accumulate(running, slab_take(slabs, final_slab), b_piece, c_cols_loc, c_count_loc)


def body(a_blocks, a_index, a_count, b_blocks, b_rows, b_cols, b_count, c_cols, c_count):
    rows_count = lax.axis_size("row")
    cols_count = lax.axis_size("col")
    layers = lax.axis_size("rep")
    spread = rows_count // cols_count
    row_at = lax.axis_index("row")
    col_at = lax.axis_index("col")
    layer_at = lax.axis_index("rep")
    own_rows = a_blocks.shape[0]
    block_size = a_blocks.shape[-1]
    retained = c_cols.shape[-1]
    c_cols_loc = c_cols[:, 0]
    c_count_loc = c_count[:, 0]
    count_of_iterations = rows_count // layers
    b_piece = (b_blocks[0, 0], b_rows[0, 0], b_cols[0, 0], b_count[0])
    slabs = (a_blocks, a_index, a_count)
    offset = layer_at * count_of_iterations
    slab_ids = jnp.arange(spread, dtype=jnp.int32)
    first_use = (slab_ids - row_at) % spread
    block_totals = (row_at + offset + first_use) // spread % cols_count
    shift_b = (spread * col_at + offset) % rows_count
    low_level = spread.bit_length() - 1
    first_slab = row_at % spread
    a_hop = 1
    b_hop = 1
    slabs = align_cols(slabs, block_totals, cols_count.bit_length() - 1)
    b_piece = align_rows(b_piece, shift_b, low_level, rows_count.bit_length() - 1)
    running = jnp.zeros((own_rows, retained, block_size, block_size), jnp.float32)
    running = walk(
        slabs,
        b_piece,
        first_slab,
        count_of_iterations,
        a_hop,
        b_hop,
        c_cols_loc,
        c_count_loc,
        running,
    )
    own_share = lax.psum_scatter(running, "rep", scatter_dimension=0, tiled=True)
    return own_share.astype(jnp.bfloat16)[:, None]


def solution(mesh):
    placed = (
        P("row", "col", None, None, None),
        P("row", "col", None),
        P("row", "col"),
        P("row", "col", None, None, None),
        P("row", "col", None),
        P("row", "col", None),
        P("row", "col"),
        P("row", "col", None),
        P("row", "col"),
    )
    return jax.shard_map(
        body,
        mesh=mesh,
        in_specs=placed,
        out_specs=P(("row", "rep"), "col", None, None, None),
        check_vma=False,
    )
```

profile of v0, /device:TPU:1, one launch (start us, length us, event | category | flops | bytes accessed | tf_op | source)
XLA Modules:
  0.0 455.9 jit_solution(1413136230126572467)
XLA Ops:
  6.6 6.5 %collective-permute-start.16 = (bf16[32,128,128]{2,1,0:T(8,128)(2,1)}, bf16[32,128,128]{2,1,0:T(8,128)(2,1)}, u32[]{:S(2)}, u32[]{:S(2)}) collective-permute-start(bf16[32,128,128]{2,1,0:T(8,128)(2,1)} %bitcast.78), channel_id=1, source_target_pairs={{0,224},{16,240},{32,0},{48,16},{64,32},{80,48},{96,64},{112,80},{... | collective-permute-start | bytes 3145736 | tf_op jit(solution)/shard_map/ppermute | solution.py:14
  14.5 2.3 copy.38
  20.7 14.5 %collective-permute-done.25 = s32[1]{0:T(128)} collective-permute-done((s32[1]{0:T(128)}, s32[1]{0:T(128)}, u32[]{:S(2)}, u32[]{:S(2)}) %collective-permute-start.25) | collective-permute-done | bytes 36 | tf_op jit(solution)/shard_map/ppermute | solution.py:14
  35.9 3.4 collective-permute-start.26
  40.1 4.3 collective-permute-start.27
  44.4 2.0 collective-permute-done.27
  47.1 2.5 collective-permute-start.14
  49.6 4.6 %collective-permute-start.19 = (s32[32]{0:T(128)S(1)}, s32[32]{0:T(128)S(1)}, u32[]{:S(2)}, u32[]{:S(2)}) collective-permute-start(s32[32]{0:T(128)S(1)} %bitcast.83), channel_id=1, source_target_pairs={{0,224},{16,240},{32,0},{48,16},{64,32},{80,48},{96,64},{112,80},{... | collective-permute-start | bytes 392 | tf_op jit(solution)/shard_map/ppermute | solution.py:14
  54.3 4.4 collective-permute-start.10
  59.6 2.1 collective-permute-start.15
  63.3 3.0 collective-permute-start.17
  68.2 3.6 collective-permute-start.24
  71.8 23.0 %collective-permute-done.20 = s32[32]{0:T(128)S(1)} collective-permute-done((s32[32]{0:T(128)S(1)}, s32[32]{0:T(128)S(1)}, u32[]{:S(2)}, u32[]{:S(2)}) %collective-permute-start.20) | collective-permute-done | bytes 160 | tf_op jit(solution)/shard_map/ppermute | solution.py:14
  96.1 4.5 collective-permute-start.18
  100.8 13.6 %collective-permute-start.9 = (bf16[8,2,2,128,128]{4,3,2,0,1:T(8,128)(2,1)S(1)}, bf16[8,2,2,128,128]{4,3,2,0,1:T(8,128)(2,1)S(1)}, u32[]{:S(2)}, u32[]{:S(2)}) collective-permute-start(bf16[8,2,2,128,128]{4,3,2,0,1:T(8,128)(2,1)S(1)} %broadcast_select_fusion.2), channel_id=1, source_target_pairs={{0,8},{2,10},{4,12},{6,14},{8,0},{10,2},{12,4},{14,6},{1,9},{3,11}... | collective-permute-start | bytes 3145736 | tf_op jit(solution)/shard_map/ppermute | solution.py:14
  114.6 20.6 %collective-permute-done.12 = s32[8,2,2]{0,2,1:T(2,128)S(1)} collective-permute-done((s32[8,2,2]{0,2,1:T(2,128)S(1)}, s32[8,2,2]{0,2,1:T(2,128)S(1)}, u32[]{:S(2)}, u32[]{:S(2)}) %collective-permute-start.12) | collective-permute-done | bytes 160 | tf_op jit(solution)/shard_map/ppermute | solution.py:14
  137.5 262.5 %while.30 = (s32[]{:T(128)}, f32[8,4,128,128]{3,1,2,0:T(4,128)S(1)}, bf16[8,2,2,128,128]{4,3,2,0,1:T(8,128)(2,1)}, s32[8,2,2]{0,2,1:T(2,128)S(1)}, s32[8,2]{0,1:...) while((s32[]{:T(128)}, ...), condition=%wide.region_3.6_spmd.clone, body=%wide.region_0.5_spmd.clone.sunk | while | flops 81008544 | bytes 18885900 | solution.py:111
  139.4 16.5 %collective-permute-start = (bf16[8,2,128,128]{3,2,1,0:T(8,128)(2,1)}, bf16[8,2,128,128]{3,2,1,0:T(8,128)(2,1)}, u32[]{:S(2)}, u32[]{:S(2)}) collective-permute-start(bf16[8,2,128,128]{3,2,1,0:T(8,128)(2,1)} %dynamic-slice_bitcast_fusion.3), channel_id=1, source_target_pairs={{0,14},{2,0},{4,2},{6,4},{8,6},{10,8},{12,10},{14,12},{1,15},{3,1}... | collective-permute-start | bytes 1572872 | tf_op jit(solution)/shard_map/while/body/eval_jaxpr/ppermute | solution.py:14
  155.9 12.4 %collective-permute-start.4 = (s32[32]{0:T(128)S(1)}, s32[32]{0:T(128)S(1)}, u32[]{:S(2)}, u32[]{:S(2)}) collective-permute-start(s32[32]{0:T(128)S(1)} %copy.89), channel_id=1, source_target_pairs={{0,240},{16,0},{32,16},{48,32},{64,48},{80,64},{96,80},{112,96},{1... | collective-permute-start | bytes 392 | tf_op jit(solution)/shard_map/while/body/eval_jaxpr/ppermute | solution.py:14
  174.5 3.8 select_add_fusion.2
  178.3 3.7 collective-permute-start.5
  182.0 3.7 collective-permute-start.6
  190.5 7.3 %collective-permute-start = (bf16[8,2,128,128]{3,2,1,0:T(8,128)(2,1)}, bf16[8,2,128,128]{3,2,1,0:T(8,128)(2,1)}, u32[]{:S(2)}, u32[]{:S(2)}) collective-permute-start(bf16[8,2,128,128]{3,2,1,0:T(8,128)(2,1)} %dynamic-slice_bitcast_fusion.3), channel_id=1, source_target_pairs={{0,14},{2,0},{4,2},{6,4},{8,6},{10,8},{12,10},{14,12},{1,15},{3,1}... | collective-permute-start | bytes 1572872 | tf_op jit(solution)/shard_map/while/body/eval_jaxpr/ppermute | solution.py:14
  197.8 6.7 %collective-permute-start.1 = (s32[8,2]{0,1:T(2,128)S(1)}, s32[8,2]{0,1:T(2,128)S(1)}, u32[]{:S(2)}, u32[]{:S(2)}) collective-permute-start(s32[8,2]{0,1:T(2,128)S(1)} %fusion.53), channel_id=1, source_target_pairs={{0,14},{2,0},{4,2},{6,4},{8,6},{10,8},{12,10},{14,12},{1,15},{3,1}... | collective-permute-start | bytes 200 | tf_op jit(solution)/shard_map/while/body/eval_jaxpr/ppermute | solution.py:14
  205.7 2.4 collective-permute-start.4
  214.1 3.8 select_add_fusion.2
  218.4 12.9 %collective-permute-start.6 = (s32[1]{0:T(128)}, s32[1]{0:T(128)}, u32[]{:S(2)}, u32[]{:S(2)}) collective-permute-start(s32[1]{0:T(128)} %copy.91), channel_id=1, source_target_pairs={{0,240},{16,0},{32,16},{48,32},{64,48},{80,64},{96,80},{112,96},{1... | collective-permute-start | bytes 20 | tf_op jit(solution)/shard_map/while/body/eval_jaxpr/ppermute | solution.py:14
  239.3 2.1 collective-permute-start.4
  247.5 3.8 select_add_fusion.2
  251.4 13.8 %collective-permute-start.6 = (s32[1]{0:T(128)}, s32[1]{0:T(128)}, u32[]{:S(2)}, u32[]{:S(2)}) collective-permute-start(s32[1]{0:T(128)} %copy.91), channel_id=1, source_target_pairs={{0,240},{16,0},{32,16},{48,32},{64,48},{80,64},{96,80},{112,96},{1... | collective-permute-start | bytes 20 | tf_op jit(solution)/shard_map/while/body/eval_jaxpr/ppermute | solution.py:14
  265.2 1.9 bitcast_dynamic-update-slice_fusion.2
  271.1 2.2 collective-permute-start.4
  279.4 3.8 select_add_fusion.2
  283.2 2.2 collective-permute-start.5
  285.4 11.7 %collective-permute-start.6 = (s32[1]{0:T(128)}, s32[1]{0:T(128)}, u32[]{:S(2)}, u32[]{:S(2)}) collective-permute-start(s32[1]{0:T(128)} %copy.91), channel_id=1, source_target_pairs={{0,240},{16,0},{32,16},{48,32},{64,48},{80,64},{96,80},{112,96},{1... | collective-permute-start | bytes 20 | tf_op jit(solution)/shard_map/while/body/eval_jaxpr/ppermute | solution.py:14
  304.2 2.1 collective-permute-start.4
  312.4 3.8 select_add_fusion.2
  317.4 12.7 %collective-permute-start.6 = (s32[1]{0:T(128)}, s32[1]{0:T(128)}, u32[]{:S(2)}, u32[]{:S(2)}) collective-permute-start(s32[1]{0:T(128)} %copy.91), channel_id=1, source_target_pairs={{0,240},{16,0},{32,16},{48,32},{64,48},{80,64},{96,80},{112,96},{1... | collective-permute-start | bytes 20 | tf_op jit(solution)/shard_map/while/body/eval_jaxpr/ppermute | solution.py:14
  337.7 2.1 collective-permute-start.4
  345.9 3.8 select_add_fusion.2
  351.6 10.9 %collective-permute-start.6 = (s32[1]{0:T(128)}, s32[1]{0:T(128)}, u32[]{:S(2)}, u32[]{:S(2)}) collective-permute-start(s32[1]{0:T(128)} %copy.91), channel_id=1, source_target_pairs={{0,240},{16,0},{32,16},{48,32},{64,48},{80,64},{96,80},{112,96},{1... | collective-permute-start | bytes 20 | tf_op jit(solution)/shard_map/while/body/eval_jaxpr/ppermute | solution.py:14
  371.2 2.3 collective-permute-start.4
  379.6 3.8 select_add_fusion.2
  383.5 2.2 collective-permute-start.5
  385.7 11.4 %collective-permute-start.6 = (s32[1]{0:T(128)}, s32[1]{0:T(128)}, u32[]{:S(2)}, u32[]{:S(2)}) collective-permute-start(s32[1]{0:T(128)} %copy.91), channel_id=1, source_target_pairs={{0,240},{16,0},{32,16},{48,32},{64,48},{80,64},{96,80},{112,96},{1... | collective-permute-start | bytes 20 | tf_op jit(solution)/shard_map/while/body/eval_jaxpr/ppermute | solution.py:14
  405.0 3.1 fusion.17
  410.3 36.7 %reduce-scatter.2.cloned.1.call-done = f32[4,4,128,128]{3,2,1,0:T(8,128)} async-done(((f32[8,4,128,128]{3,2,1,0:T(8,128)}), f32[4,4,128,128]{3,2,1,0:T(8,128)}) %reduce-scatter.2.cloned.1.call-update) | async-done | bytes 1048592 | tf_op jit(solution)/shard_map/reduce_scatter | solution.py:157
  447.0 2.1 convert_bitcast_fusion
  (361 shorter events, 107.5 us)
Async XLA Ops:
  6.6 440.4 %reduce-scatter.2.cloned.1.call-start = ((), (), s32[]{:S(2)}) async-start(), calls=%async_computation.1 | async-start | bytes 3145728 | tf_op jit(solution)/shard_map/reduce_scatter | solution.py:157
  6.6 55.1 %collective-permute-start.16 = (bf16[32,128,128]{2,1,0:T(8,128)(2,1)}, bf16[32,128,128]{2,1,0:T(8,128)(2,1)}, u32[]{:S(2)}, u32[]{:S(2)}) collective-permute-start(bf16[32,128,128]{2,1,0:T(8,128)(2,1)} %bitcast.78), channel_id=1, source_target_pairs={{0,224},{16,240},{32,0},{48,16},{64,32},{80,48},{96,64},{112,80},{... | collective-permute-start | bytes 3145736 | tf_op jit(solution)/shard_map/ppermute | solution.py:14
  13.1 22.1 %collective-permute-start.25 = (s32[1]{0:T(128)}, s32[1]{0:T(128)}, u32[]{:S(2)}, u32[]{:S(2)}) collective-permute-start(s32[1]{0:T(128)} %bitcast.6), channel_id=1, source_target_pairs={{0,224},{16,240},{32,0},{48,16},{64,32},{80,48},{96,64},{112,80},{... | collective-permute-start | bytes 20 | tf_op jit(solution)/shard_map/ppermute | solution.py:14
  13.8 44.9 %collective-permute-start.22 = (s32[32]{0:T(128)}, s32[32]{0:T(128)S(1)}, u32[]{:S(2)}, u32[]{:S(2)}) collective-permute-start(s32[32]{0:T(128)} %bitcast.82), channel_id=1, source_target_pairs={{0,224},{16,240},{32,0},{48,16},{64,32},{80,48},{96,64},{112,80},{... | collective-permute-start | bytes 392 | tf_op jit(solution)/shard_map/ppermute | solution.py:14
  16.8 49.5 %collective-permute-start.7 = (bf16[8,2,2,128,128]{4,3,2,0,1:T(8,128)(2,1)}, bf16[8,2,2,128,128]{4,3,2,0,1:T(8,128)(2,1)}, u32[]{:S(2)}, u32[]{:S(2)}) collective-permute-start(bf16[8,2,2,128,128]{4,3,2,0,1:T(8,128)(2,1)} %copy.38), channel_id=1, source_target_pairs={{0,14},{2,0},{4,2},{6,4},{8,6},{10,8},{12,10},{14,12},{1,15},{3,1}... | collective-permute-start | bytes 3145736 | tf_op jit(solution)/shard_map/ppermute | solution.py:14
  19.3 27.7 %collective-permute-start.13 = (s32[8,2]{0,1:T(2,128)S(1)}, s32[8,2]{0,1:T(2,128)S(1)}, u32[]{:S(2)}, u32[]{:S(2)}) collective-permute-start(s32[8,2]{0,1:T(2,128)S(1)} %copy-done.3), channel_id=1, source_target_pairs={{0,14},{2,0},{4,2},{6,4},{8,6},{10,8},{12,10},{14,12},{1,15},{3,1}... | collective-permute-start | bytes 200 | tf_op jit(solution)/shard_map/ppermute | solution.py:14
  49.6 18.2 %collective-permute-start.19 = (s32[32]{0:T(128)S(1)}, s32[32]{0:T(128)S(1)}, u32[]{:S(2)}, u32[]{:S(2)}) collective-permute-start(s32[32]{0:T(128)S(1)} %bitcast.83), channel_id=1, source_target_pairs={{0,224},{16,240},{32,0},{48,16},{64,32},{80,48},{96,64},{112,80},{... | collective-permute-start | bytes 392 | tf_op jit(solution)/shard_map/ppermute | solution.py:14
  63.3 32.7 %collective-permute-start.17 = (bf16[32,128,128]{2,1,0:T(8,128)(2,1)S(1)}, bf16[32,128,128]{2,1,0:T(8,128)(2,1)S(1)}, u32[]{:S(2)}, u32[]{:S(2)}) collective-permute-start(bf16[32,128,128]{2,1,0:T(8,128)(2,1)S(1)} %broadcast_select_fusion.4), channel_id=1, source_target_pairs={{0,192},{16,208},{32,224},{48,240},{64,0},{80,16},{96,32},{112,48}... | collective-permute-start | bytes 3145736 | tf_op jit(solution)/shard_map/ppermute | solution.py:14
  67.7 32.9 %collective-permute-start.8 = (bf16[8,2,2,128,128]{4,3,2,0,1:T(8,128)(2,1)S(1)}, bf16[8,2,2,128,128]{4,3,2,0,1:T(8,128)(2,1)S(1)}, u32[]{:S(2)}, u32[]{:S(2)}) collective-permute-start(bf16[8,2,2,128,128]{4,3,2,0,1:T(8,128)(2,1)S(1)} %broadcast_select_fusion.1), channel_id=1, source_target_pairs={{0,12},{2,14},{4,0},{6,2},{8,4},{10,6},{12,8},{14,10},{1,13},{3,15... | collective-permute-start | bytes 3145736 | tf_op jit(solution)/shard_map/ppermute | solution.py:14
  67.8 27.0 %collective-permute-start.20 = (s32[32]{0:T(128)S(1)}, s32[32]{0:T(128)S(1)}, u32[]{:S(2)}, u32[]{:S(2)}) collective-permute-start(s32[32]{0:T(128)S(1)} %broadcast_select_fusion.14), channel_id=1, source_target_pairs={{0,192},{16,208},{32,224},{48,240},{64,0},{80,16},{96,32},{112,48}... | collective-permute-start | bytes 392 | tf_op jit(solution)/shard_map/ppermute | solution.py:14
  68.0 46.4 %collective-permute-start.11 = (s32[8,2,2]{0,2,1:T(2,128)S(1)}, s32[8,2,2]{0,2,1:T(2,128)S(1)}, u32[]{:S(2)}, u32[]{:S(2)}) collective-permute-start(s32[8,2,2]{0,2,1:T(2,128)S(1)} %broadcast_select_fusion.7), channel_id=1, source_target_pairs={{0,12},{2,14},{4,0},{6,2},{8,4},{10,6},{12,8},{14,10},{1,13},{3,15... | collective-permute-start | bytes 392 | tf_op jit(solution)/shard_map/ppermute | solution.py:14
  68.2 46.3 %collective-permute-start.24 = (s32[32]{0:T(128)S(1)}, s32[32]{0:T(128)S(1)}, u32[]{:S(2)}, u32[]{:S(2)}) collective-permute-start(s32[32]{0:T(128)S(1)} %broadcast_select_fusion.15), channel_id=1, source_target_pairs={{0,128},{16,144},{32,160},{48,176},{64,192},{80,208},{96,224},{112... | collective-permute-start | bytes 392 | tf_op jit(solution)/shard_map/ppermute | solution.py:14
  94.9 19.7 %collective-permute-start.21 = (s32[32]{0:T(128)S(1)}, s32[32]{0:T(128)S(1)}, u32[]{:S(2)}, u32[]{:S(2)}) collective-permute-start(s32[32]{0:T(128)S(1)} %broadcast_select_fusion.16), channel_id=1, source_target_pairs={{0,128},{16,144},{32,160},{48,176},{64,192},{80,208},{96,224},{112... | collective-permute-start | bytes 392 | tf_op jit(solution)/shard_map/ppermute | solution.py:14
  96.1 39.1 %collective-permute-start.18 = (bf16[32,128,128]{2,1,0:T(8,128)(2,1)S(1)}, bf16[32,128,128]{2,1,0:T(8,128)(2,1)S(1)}, u32[]{:S(2)}, u32[]{:S(2)}) collective-permute-start(bf16[32,128,128]{2,1,0:T(8,128)(2,1)S(1)} %broadcast_select_fusion.5), channel_id=1, source_target_pairs={{0,128},{16,144},{32,160},{48,176},{64,192},{80,208},{96,224},{112... | collective-permute-start | bytes 3145736 | tf_op jit(solution)/shard_map/ppermute | solution.py:14
  100.8 35.5 %collective-permute-start.9 = (bf16[8,2,2,128,128]{4,3,2,0,1:T(8,128)(2,1)S(1)}, bf16[8,2,2,128,128]{4,3,2,0,1:T(8,128)(2,1)S(1)}, u32[]{:S(2)}, u32[]{:S(2)}) collective-permute-start(bf16[8,2,2,128,128]{4,3,2,0,1:T(8,128)(2,1)S(1)} %broadcast_select_fusion.2), channel_id=1, source_target_pairs={{0,8},{2,10},{4,12},{6,14},{8,0},{10,2},{12,4},{14,6},{1,9},{3,11}... | collective-permute-start | bytes 3145736 | tf_op jit(solution)/shard_map/ppermute | solution.py:14
  114.5 20.7 %collective-permute-start.12 = (s32[8,2,2]{0,2,1:T(2,128)S(1)}, s32[8,2,2]{0,2,1:T(2,128)S(1)}, u32[]{:S(2)}, u32[]{:S(2)}) collective-permute-start(s32[8,2,2]{0,2,1:T(2,128)S(1)} %broadcast_select_fusion.8), channel_id=1, source_target_pairs={{0,8},{2,10},{4,12},{6,14},{8,0},{10,2},{12,4},{14,6},{1,9},{3,11}... | collective-permute-start | bytes 392 | tf_op jit(solution)/shard_map/ppermute | solution.py:14
  139.4 46.4 %collective-permute-start = (bf16[8,2,128,128]{3,2,1,0:T(8,128)(2,1)}, bf16[8,2,128,128]{3,2,1,0:T(8,128)(2,1)}, u32[]{:S(2)}, u32[]{:S(2)}) collective-permute-start(bf16[8,2,128,128]{3,2,1,0:T(8,128)(2,1)} %dynamic-slice_bitcast_fusion.3), channel_id=1, source_target_pairs={{0,14},{2,0},{4,2},{6,4},{8,6},{10,8},{12,10},{14,12},{1,15},{3,1}... | collective-permute-start | bytes 1572872 | tf_op jit(solution)/shard_map/while/body/eval_jaxpr/ppermute | solution.py:14
  155.8 26.2 %collective-permute-start.1 = (s32[8,2]{0,1:T(2,128)S(1)}, s32[8,2]{0,1:T(2,128)S(1)}, u32[]{:S(2)}, u32[]{:S(2)}) collective-permute-start(s32[8,2]{0,1:T(2,128)S(1)} %fusion.53), channel_id=1, source_target_pairs={{0,14},{2,0},{4,2},{6,4},{8,6},{10,8},{12,10},{14,12},{1,15},{3,1}... | collective-permute-start | bytes 200 | tf_op jit(solution)/shard_map/while/body/eval_jaxpr/ppermute | solution.py:14
  155.8 22.4 %collective-permute-start.2 = (s32[8]{0:T(128)S(1)}, s32[8]{0:T(128)S(1)}, u32[]{:S(2)}, u32[]{:S(2)}) collective-permute-start(s32[8]{0:T(128)S(1)} %fusion.54), channel_id=1, source_target_pairs={{0,14},{2,0},{4,2},{6,4},{8,6},{10,8},{12,10},{14,12},{1,15},{3,1}... | collective-permute-start | bytes 104 | tf_op jit(solution)/shard_map/while/body/eval_jaxpr/ppermute | solution.py:14
  155.9 32.0 %collective-permute-start.4 = (s32[32]{0:T(128)S(1)}, s32[32]{0:T(128)S(1)}, u32[]{:S(2)}, u32[]{:S(2)}) collective-permute-start(s32[32]{0:T(128)S(1)} %copy.89), channel_id=1, source_target_pairs={{0,240},{16,0},{32,16},{48,32},{64,48},{80,64},{96,80},{112,96},{1... | collective-permute-start | bytes 392 | tf_op jit(solution)/shard_map/while/body/eval_jaxpr/ppermute | solution.py:14
  169.5 18.4 %collective-permute-start.3 = (bf16[32,128,128]{2,1,0:T(8,128)(2,1)S(1)}, bf16[32,128,128]{2,1,0:T(8,128)(2,1)}, u32[]{:S(2)}, u32[]{:S(2)}) collective-permute-start(bf16[32,128,128]{2,1,0:T(8,128)(2,1)S(1)} %copy.88), channel_id=1, source_target_pairs={{0,240},{16,0},{32,16},{48,32},{64,48},{80,64},{96,80},{112,96},{1... | collective-permute-start | bytes 3145736 | tf_op jit(solution)/shard_map/while/body/eval_jaxpr/ppermute | solution.py:14
  190.5 40.9 %collective-permute-start = (bf16[8,2,128,128]{3,2,1,0:T(8,128)(2,1)}, bf16[8,2,128,128]{3,2,1,0:T(8,128)(2,1)}, u32[]{:S(2)}, u32[]{:S(2)}) collective-permute-start(bf16[8,2,128,128]{3,2,1,0:T(8,128)(2,1)} %dynamic-slice_bitcast_fusion.3), channel_id=1, source_target_pairs={{0,14},{2,0},{4,2},{6,4},{8,6},{10,8},{12,10},{14,12},{1,15},{3,1}... | collective-permute-start | bytes 1572872 | tf_op jit(solution)/shard_map/while/body/eval_jaxpr/ppermute | solution.py:14
  197.8 20.6 %collective-permute-start.1 = (s32[8,2]{0,1:T(2,128)S(1)}, s32[8,2]{0,1:T(2,128)S(1)}, u32[]{:S(2)}, u32[]{:S(2)}) collective-permute-start(s32[8,2]{0,1:T(2,128)S(1)} %fusion.53), channel_id=1, source_target_pairs={{0,14},{2,0},{4,2},{6,4},{8,6},{10,8},{12,10},{14,12},{1,15},{3,1}... | collective-permute-start | bytes 200 | tf_op jit(solution)/shard_map/while/body/eval_jaxpr/ppermute | solution.py:14
  205.7 27.6 %collective-permute-start.4 = (s32[32]{0:T(128)S(1)}, s32[32]{0:T(128)S(1)}, u32[]{:S(2)}, u32[]{:S(2)}) collective-permute-start(s32[32]{0:T(128)S(1)} %copy.89), channel_id=1, source_target_pairs={{0,240},{16,0},{32,16},{48,32},{64,48},{80,64},{96,80},{112,96},{1... | collective-permute-start | bytes 392 | tf_op jit(solution)/shard_map/while/body/eval_jaxpr/ppermute | solution.py:14
  209.3 24.0 %collective-permute-start.3 = (bf16[32,128,128]{2,1,0:T(8,128)(2,1)S(1)}, bf16[32,128,128]{2,1,0:T(8,128)(2,1)}, u32[]{:S(2)}, u32[]{:S(2)}) collective-permute-start(bf16[32,128,128]{2,1,0:T(8,128)(2,1)S(1)} %copy.88), channel_id=1, source_target_pairs={{0,240},{16,0},{32,16},{48,32},{64,48},{80,64},{96,80},{112,96},{1... | collective-permute-start | bytes 3145736 | tf_op jit(solution)/shard_map/while/body/eval_jaxpr/ppermute | solution.py:14
  217.9 15.4 %collective-permute-start.5 = (s32[32]{0:T(128)S(1)}, s32[32]{0:T(128)S(1)}, u32[]{:S(2)}, u32[]{:S(2)}) collective-permute-start(s32[32]{0:T(128)S(1)} %copy.90), channel_id=1, source_target_pairs={{0,240},{16,0},{32,16},{48,32},{64,48},{80,64},{96,80},{112,96},{1... | collective-permute-start | bytes 392 | tf_op jit(solution)/shard_map/while/body/eval_jaxpr/ppermute | solution.py:14
  235.9 29.3 %collective-permute-start = (bf16[8,2,128,128]{3,2,1,0:T(8,128)(2,1)}, bf16[8,2,128,128]{3,2,1,0:T(8,128)(2,1)}, u32[]{:S(2)}, u32[]{:S(2)}) collective-permute-start(bf16[8,2,128,128]{3,2,1,0:T(8,128)(2,1)} %dynamic-slice_bitcast_fusion.3), channel_id=1, source_target_pairs={{0,14},{2,0},{4,2},{6,4},{8,6},{10,8},{12,10},{14,12},{1,15},{3,1}... | collective-permute-start | bytes 1572872 | tf_op jit(solution)/shard_map/while/body/eval_jaxpr/ppermute | solution.py:14
  239.3 27.9 %collective-permute-start.4 = (s32[32]{0:T(128)S(1)}, s32[32]{0:T(128)S(1)}, u32[]{:S(2)}, u32[]{:S(2)}) collective-permute-start(s32[32]{0:T(128)S(1)} %copy.89), channel_id=1, source_target_pairs={{0,240},{16,0},{32,16},{48,32},{64,48},{80,64},{96,80},{112,96},{1... | collective-permute-start | bytes 392 | tf_op jit(solution)/shard_map/while/body/eval_jaxpr/ppermute | solution.py:14
  242.6 24.5 %collective-permute-start.3 = (bf16[32,128,128]{2,1,0:T(8,128)(2,1)S(1)}, bf16[32,128,128]{2,1,0:T(8,128)(2,1)}, u32[]{:S(2)}, u32[]{:S(2)}) collective-permute-start(bf16[32,128,128]{2,1,0:T(8,128)(2,1)S(1)} %copy.88), channel_id=1, source_target_pairs={{0,240},{16,0},{32,16},{48,32},{64,48},{80,64},{96,80},{112,96},{1... | collective-permute-start | bytes 3145736 | tf_op jit(solution)/shard_map/while/body/eval_jaxpr/ppermute | solution.py:14
  251.3 15.8 %collective-permute-start.5 = (s32[32]{0:T(128)S(1)}, s32[32]{0:T(128)S(1)}, u32[]{:S(2)}, u32[]{:S(2)}) collective-permute-start(s32[32]{0:T(128)S(1)} %copy.90), channel_id=1, source_target_pairs={{0,240},{16,0},{32,16},{48,32},{64,48},{80,64},{96,80},{112,96},{1... | collective-permute-start | bytes 392 | tf_op jit(solution)/shard_map/while/body/eval_jaxpr/ppermute | solution.py:14
  251.4 15.7 %collective-permute-start.6 = (s32[1]{0:T(128)}, s32[1]{0:T(128)}, u32[]{:S(2)}, u32[]{:S(2)}) collective-permute-start(s32[1]{0:T(128)} %copy.91), channel_id=1, source_target_pairs={{0,240},{16,0},{32,16},{48,32},{64,48},{80,64},{96,80},{112,96},{1... | collective-permute-start | bytes 20 | tf_op jit(solution)/shard_map/while/body/eval_jaxpr/ppermute | solution.py:14
  269.8 27.4 %collective-permute-start = (bf16[8,2,128,128]{3,2,1,0:T(8,128)(2,1)}, bf16[8,2,128,128]{3,2,1,0:T(8,128)(2,1)}, u32[]{:S(2)}, u32[]{:S(2)}) collective-permute-start(bf16[8,2,128,128]{3,2,1,0:T(8,128)(2,1)} %dynamic-slice_bitcast_fusion.3), channel_id=1, source_target_pairs={{0,14},{2,0},{4,2},{6,4},{8,6},{10,8},{12,10},{14,12},{1,15},{3,1}... | collective-permute-start | bytes 1572872 | tf_op jit(solution)/shard_map/while/body/eval_jaxpr/ppermute | solution.py:14
  271.1 28.0 %collective-permute-start.4 = (s32[32]{0:T(128)S(1)}, s32[32]{0:T(128)S(1)}, u32[]{:S(2)}, u32[]{:S(2)}) collective-permute-start(s32[32]{0:T(128)S(1)} %copy.89), channel_id=1, source_target_pairs={{0,240},{16,0},{32,16},{48,32},{64,48},{80,64},{96,80},{112,96},{1... | collective-permute-start | bytes 392 | tf_op jit(solution)/shard_map/while/body/eval_jaxpr/ppermute | solution.py:14
  274.6 24.5 %collective-permute-start.3 = (bf16[32,128,128]{2,1,0:T(8,128)(2,1)S(1)}, bf16[32,128,128]{2,1,0:T(8,128)(2,1)}, u32[]{:S(2)}, u32[]{:S(2)}) collective-permute-start(bf16[32,128,128]{2,1,0:T(8,128)(2,1)S(1)} %copy.88), channel_id=1, source_target_pairs={{0,240},{16,0},{32,16},{48,32},{64,48},{80,64},{96,80},{112,96},{1... | collective-permute-start | bytes 3145736 | tf_op jit(solution)/shard_map/while/body/eval_jaxpr/ppermute | solution.py:14
  283.2 15.8 %collective-permute-start.5 = (s32[32]{0:T(128)S(1)}, s32[32]{0:T(128)S(1)}, u32[]{:S(2)}, u32[]{:S(2)}) collective-permute-start(s32[32]{0:T(128)S(1)} %copy.90), channel_id=1, source_target_pairs={{0,240},{16,0},{32,16},{48,32},{64,48},{80,64},{96,80},{112,96},{1... | collective-permute-start | bytes 392 | tf_op jit(solution)/shard_map/while/body/eval_jaxpr/ppermute | solution.py:14
  301.7 28.5 %collective-permute-start = (bf16[8,2,128,128]{3,2,1,0:T(8,128)(2,1)}, bf16[8,2,128,128]{3,2,1,0:T(8,128)(2,1)}, u32[]{:S(2)}, u32[]{:S(2)}) collective-permute-start(bf16[8,2,128,128]{3,2,1,0:T(8,128)(2,1)} %dynamic-slice_bitcast_fusion.3), channel_id=1, source_target_pairs={{0,14},{2,0},{4,2},{6,4},{8,6},{10,8},{12,10},{14,12},{1,15},{3,1}... | collective-permute-start | bytes 1572872 | tf_op jit(solution)/shard_map/while/body/eval_jaxpr/ppermute | solution.py:14
  304.2 27.9 %collective-permute-start.4 = (s32[32]{0:T(128)S(1)}, s32[32]{0:T(128)S(1)}, u32[]{:S(2)}, u32[]{:S(2)}) collective-permute-start(s32[32]{0:T(128)S(1)} %copy.89), channel_id=1, source_target_pairs={{0,240},{16,0},{32,16},{48,32},{64,48},{80,64},{96,80},{112,96},{1... | collective-permute-start | bytes 392 | tf_op jit(solution)/shard_map/while/body/eval_jaxpr/ppermute | solution.py:14
  307.6 24.5 %collective-permute-start.3 = (bf16[32,128,128]{2,1,0:T(8,128)(2,1)S(1)}, bf16[32,128,128]{2,1,0:T(8,128)(2,1)}, u32[]{:S(2)}, u32[]{:S(2)}) collective-permute-start(bf16[32,128,128]{2,1,0:T(8,128)(2,1)S(1)} %copy.88), channel_id=1, source_target_pairs={{0,240},{16,0},{32,16},{48,32},{64,48},{80,64},{96,80},{112,96},{1... | collective-permute-start | bytes 3145736 | tf_op jit(solution)/shard_map/while/body/eval_jaxpr/ppermute | solution.py:14
  316.3 15.8 %collective-permute-start.5 = (s32[32]{0:T(128)S(1)}, s32[32]{0:T(128)S(1)}, u32[]{:S(2)}, u32[]{:S(2)}) collective-permute-start(s32[32]{0:T(128)S(1)} %copy.90), channel_id=1, source_target_pairs={{0,240},{16,0},{32,16},{48,32},{64,48},{80,64},{96,80},{112,96},{1... | collective-permute-start | bytes 392 | tf_op jit(solution)/shard_map/while/body/eval_jaxpr/ppermute | solution.py:14
  334.7 27.8 %collective-permute-start = (bf16[8,2,128,128]{3,2,1,0:T(8,128)(2,1)}, bf16[8,2,128,128]{3,2,1,0:T(8,128)(2,1)}, u32[]{:S(2)}, u32[]{:S(2)}) collective-permute-start(bf16[8,2,128,128]{3,2,1,0:T(8,128)(2,1)} %dynamic-slice_bitcast_fusion.3), channel_id=1, source_target_pairs={{0,14},{2,0},{4,2},{6,4},{8,6},{10,8},{12,10},{14,12},{1,15},{3,1}... | collective-permute-start | bytes 1572872 | tf_op jit(solution)/shard_map/while/body/eval_jaxpr/ppermute | solution.py:14
  335.9 15.7 %collective-permute-start.1 = (s32[8,2]{0,1:T(2,128)S(1)}, s32[8,2]{0,1:T(2,128)S(1)}, u32[]{:S(2)}, u32[]{:S(2)}) collective-permute-start(s32[8,2]{0,1:T(2,128)S(1)} %fusion.53), channel_id=1, source_target_pairs={{0,14},{2,0},{4,2},{6,4},{8,6},{10,8},{12,10},{14,12},{1,15},{3,1}... | collective-permute-start | bytes 200 | tf_op jit(solution)/shard_map/while/body/eval_jaxpr/ppermute | solution.py:14
  337.7 27.2 %collective-permute-start.4 = (s32[32]{0:T(128)S(1)}, s32[32]{0:T(128)S(1)}, u32[]{:S(2)}, u32[]{:S(2)}) collective-permute-start(s32[32]{0:T(128)S(1)} %copy.89), channel_id=1, source_target_pairs={{0,240},{16,0},{32,16},{48,32},{64,48},{80,64},{96,80},{112,96},{1... | collective-permute-start | bytes 392 | tf_op jit(solution)/shard_map/while/body/eval_jaxpr/ppermute | solution.py:14
  341.1 23.9 %collective-permute-start.3 = (bf16[32,128,128]{2,1,0:T(8,128)(2,1)S(1)}, bf16[32,128,128]{2,1,0:T(8,128)(2,1)}, u32[]{:S(2)}, u32[]{:S(2)}) collective-permute-start(bf16[32,128,128]{2,1,0:T(8,128)(2,1)S(1)} %copy.88), channel_id=1, source_target_pairs={{0,240},{16,0},{32,16},{48,32},{64,48},{80,64},{96,80},{112,96},{1... | collective-permute-start | bytes 3145736 | tf_op jit(solution)/shard_map/while/body/eval_jaxpr/ppermute | solution.py:14
  367.6 29.5 %collective-permute-start = (bf16[8,2,128,128]{3,2,1,0:T(8,128)(2,1)}, bf16[8,2,128,128]{3,2,1,0:T(8,128)(2,1)}, u32[]{:S(2)}, u32[]{:S(2)}) collective-permute-start(bf16[8,2,128,128]{3,2,1,0:T(8,128)(2,1)} %dynamic-slice_bitcast_fusion.3), channel_id=1, source_target_pairs={{0,14},{2,0},{4,2},{6,4},{8,6},{10,8},{12,10},{14,12},{1,15},{3,1}... | collective-permute-start | bytes 1572872 | tf_op jit(solution)/shard_map/while/body/eval_jaxpr/ppermute | solution.py:14
  369.4 16.3 %collective-permute-start.1 = (s32[8,2]{0,1:T(2,128)S(1)}, s32[8,2]{0,1:T(2,128)S(1)}, u32[]{:S(2)}, u32[]{:S(2)}) collective-permute-start(s32[8,2]{0,1:T(2,128)S(1)} %fusion.53), channel_id=1, source_target_pairs={{0,14},{2,0},{4,2},{6,4},{8,6},{10,8},{12,10},{14,12},{1,15},{3,1}... | collective-permute-start | bytes 200 | tf_op jit(solution)/shard_map/while/body/eval_jaxpr/ppermute | solution.py:14
  371.2 28.0 %collective-permute-start.4 = (s32[32]{0:T(128)S(1)}, s32[32]{0:T(128)S(1)}, u32[]{:S(2)}, u32[]{:S(2)}) collective-permute-start(s32[32]{0:T(128)S(1)} %copy.89), channel_id=1, source_target_pairs={{0,240},{16,0},{32,16},{48,32},{64,48},{80,64},{96,80},{112,96},{1... | collective-permute-start | bytes 392 | tf_op jit(solution)/shard_map/while/body/eval_jaxpr/ppermute | solution.py:14
  374.8 24.5 %collective-permute-start.3 = (bf16[32,128,128]{2,1,0:T(8,128)(2,1)S(1)}, bf16[32,128,128]{2,1,0:T(8,128)(2,1)}, u32[]{:S(2)}, u32[]{:S(2)}) collective-permute-start(bf16[32,128,128]{2,1,0:T(8,128)(2,1)S(1)} %copy.88), channel_id=1, source_target_pairs={{0,240},{16,0},{32,16},{48,32},{64,48},{80,64},{96,80},{112,96},{1... | collective-permute-start | bytes 3145736 | tf_op jit(solution)/shard_map/while/body/eval_jaxpr/ppermute | solution.py:14
  383.5 15.8 %collective-permute-start.5 = (s32[32]{0:T(128)S(1)}, s32[32]{0:T(128)S(1)}, u32[]{:S(2)}, u32[]{:S(2)}) collective-permute-start(s32[32]{0:T(128)S(1)} %copy.90), channel_id=1, source_target_pairs={{0,240},{16,0},{32,16},{48,32},{64,48},{80,64},{96,80},{112,96},{1... | collective-permute-start | bytes 392 | tf_op jit(solution)/shard_map/while/body/eval_jaxpr/ppermute | solution.py:14
  (30 other events, 492.8 us)
Sparse Core Ops, SparseCore 0:
  410.4 36.4 reduce-scatter.1
where the time goes:
time: 457 us; the launch traced here: 456 us
  starting transfers between devices  219 us (48%)
  waiting for transfers between devices  98.6 us (22%)
  local copies, waits for them, and re-layouts  61.9 us (14%)
  matrix products  42.2 us (9%)
  between operations  16.3 us (4%)
  other arithmetic  12.6 us (3%)
  loops' own time  5.53 us (1%)
    ppermute x70, starting transfers between devices, from_behind(): return lax.ppermute(value, axis, pairs)  219 us
    ppermute x70, waiting for transfers between devices, from_behind(): return lax.ppermute(value, axis, pairs)  61.9 us
    reduce_scatter x1, waiting for transfers between devices, body(): lax.psum_scatter(running, 'rep', scatter_dimension=0, tiled=True)  36.7 us
    dot_general x8, matrix products, accumulate(): jnp.einsum('ias,iaxz->isxz', landing.astype(jnp.float32), products, preci...  29.7 us
    dynamic_update_slice x21, local copies, waits for them, and re-layouts, slab_put(): lax.dynamic_update_index_in_dim(member, update, slab_no, 1)  13.6 us
    squeeze x7, local copies, waits for them, and re-layouts, slab_take(): lax.dynamic_index_in_dim(member, slab_no, 1, keepdims=False)  13.2 us
    dot_general x8, matrix products, accumulate(): jnp.einsum('iaxy,iayz->iaxz', a_blk, picked, preferred_element_type=jnp.f...  12.5 us
    gather x8, local copies, waits for them, and re-layouts, accumulate(): picked = jnp.take(b_blk, where_b, axis=0)  11.8 us
  transfers between devices with their start and end apart: 71, of which 9 were waited for; matrix products, arithmetic and copies ran while one was open for 20% of the time, Pallas kernels for 0%

commit v1 on v0

v1 whole, which is shorter than its diff:
```python
import functools

import jax
import jax.numpy as jnp
from jax import lax
from jax.experimental import pallas as pl
from jax.experimental.pallas import tpu as pltpu
from jax.sharding import Mesh
from jax.sharding import PartitionSpec as P

NZ, NYL, NX, NCORE, NREP = 8, 2, 4, 2, 2
AXES = ("z", "yl", "x", "core", "rep")
COL = ("x", "core")
BS, SA, SC, MB = 128, 2, 4, 32
ROWS = 4
PAIR = ROWS * 2 * SA
CAP = 10
HDR = 16
LANES = 128


def y_index(y):
    return (y % NYL) * NREP + y // NYL


def shift_y(value, steps):
    n = NYL * NREP
    return lax.ppermute(value, ("yl", "rep"), [(y_index(y), y_index((y + steps) % n)) for y in range(n)])


def spread(value, axis_name):
    return lax.all_to_all(value, axis_name, 0, 0)


def pack_kernel(lo, size, meta, own, other, b_own, b_low, b_high, out, held, codes, scalars, sems):
    copies = [
        pltpu.make_async_copy(b_own, held.at[pl.ds(0, MB)], sems.at[0]),
        pltpu.make_async_copy(b_low, held.at[pl.ds(MB, MB // 2)], sems.at[1]),
        pltpu.make_async_copy(b_high, held.at[pl.ds(MB + MB // 2, MB // 2)], sems.at[2]),
    ]
    for copy in copies:
        copy.start()
    yl = lax.axis_index("yl")
    lane = lax.broadcasted_iota(jnp.int32, (NZ, LANES), 1)
    is_own = ((lane >> 1) & 1) == yl
    wanted = meta[:, :LANES]
    slot = jnp.zeros((NZ, LANES), jnp.int32)
    target = jnp.full((NZ, LANES), -5, jnp.int32)
    for m in range(MB):
        hit = wanted == jnp.where(is_own, own[0, m], other[0, m])
        slot = jnp.where(hit, m, slot)
        target = jnp.where(hit, jnp.where(is_own, own[1, m], other[1, m]), target)
    code = jnp.full((NZ, LANES), -1, jnp.int32)
    for s in range(SC):
        code = jnp.where(meta[:, (s + 1) * LANES : (s + 2) * LANES] == target, slot * SC + s, code)
    codes[...] = code
    to_scalars = pltpu.make_async_copy(codes, scalars, sems.at[3])
    to_scalars.start()
    head = jnp.concatenate([code, jnp.full((HDR - NZ, LANES), -1, jnp.int32)], axis=0)
    head = head.astype(jnp.float32).astype(jnp.bfloat16)
    for z in range(NZ):
        out[z, pl.ds(size * BS, HDR), :] = head
    to_scalars.wait()
    for copy in copies:
        copy.wait()

    def per_z(z, carry):
        def step(t, count):
            code = scalars[z, t]
            hit = code >= 0

            @pl.when(hit & (count >= lo) & (count < lo + size))
            def _():
                block = (code >> 2) + jnp.where(((t >> 1) & 1) == yl, 0, MB)
                out[z, pl.ds(pl.multiple_of((count - lo) * BS, BS), BS), :] = held[block]

            return count + hit.astype(jnp.int32)

        lax.fori_loop(0, PAIR, step, jnp.int32(0))
        return carry

    lax.fori_loop(0, NZ, per_z, 0)


def pack(meta, own, other, b_own, b_low, b_high, lo, size):
    smem, vmem, hbm = (pl.BlockSpec(memory_space=m) for m in (pltpu.SMEM, pltpu.VMEM, pl.ANY))
    return pl.pallas_call(
        functools.partial(pack_kernel, lo, size),
        out_shape=jax.ShapeDtypeStruct((NZ, size * BS + HDR, BS), jnp.bfloat16),
        in_specs=[vmem, smem, smem, hbm, hbm, hbm],
        out_specs=vmem,
        scratch_shapes=[
            pltpu.VMEM((2 * MB, BS, BS), jnp.bfloat16),
            pltpu.VMEM((NZ, LANES), jnp.int32),
            pltpu.SMEM((NZ, LANES), jnp.int32),
            pltpu.SemaphoreType.DMA((4,)),
        ],
        compiler_params=pltpu.CompilerParams(vmem_limit_bytes=24 * 2**20),
        name="pack",
    )(meta, own, other, b_own, b_low, b_high)


def consume_kernel(parts, a_all, *rest):
    msgs, (out, longest, total, codes, scalars, sem) = rest[: len(parts)], rest[len(parts) :]
    me = lax.axis_index("z")
    row = lax.broadcasted_iota(jnp.int32, (HDR, LANES), 0)
    most = jnp.zeros((HDR, 1), jnp.int32)
    for z in range(NZ):
        head = msgs[0][z, pl.ds(parts[0][1] * BS, HDR), :].astype(jnp.float32).astype(jnp.int32)
        codes[pl.ds(z, 1), :] = jnp.sum(jnp.where(row == me, head, 0), axis=0, keepdims=True)
        most = jnp.maximum(most, jnp.sum((head >= 0).astype(jnp.int32), axis=1, keepdims=True))
    to_scalars = pltpu.make_async_copy(codes, scalars, sem)
    to_scalars.start()
    longest[...] = jnp.broadcast_to(jnp.max(most, axis=0, keepdims=True), longest.shape)
    total[...] = jnp.zeros_like(total)
    to_scalars.wait()

    def per_z(z, carry):
        def step(t, count):
            code = scalars[z, t]
            hit = code >= 0
            place = (t >> 2) * SC + (code & 3)
            for (lo, size), msg in zip(parts, msgs):

                @pl.when(hit & (count >= lo) & (count < lo + size))
                def _(lo=lo, msg=msg):
                    block = msg[z, pl.ds(pl.multiple_of((count - lo) * BS, BS), BS), :]
                    total[place] += jnp.dot(a_all[z, t], block, preferred_element_type=jnp.float32)

            return count + hit.astype(jnp.int32)

        lax.fori_loop(0, PAIR, step, jnp.int32(0))
        return carry

    lax.fori_loop(0, NZ, per_z, 0)
    out[...] = total[...].astype(out.dtype)


def consume(a_all, msgs, parts):
    vmem = pl.BlockSpec(memory_space=pltpu.VMEM)
    return pl.pallas_call(
        functools.partial(consume_kernel, parts),
        out_shape=(
            jax.ShapeDtypeStruct((ROWS * SC, BS, BS), jnp.bfloat16),
            jax.ShapeDtypeStruct((8, LANES), jnp.int32),
        ),
        in_specs=[vmem] * (1 + len(msgs)),
        out_specs=(vmem, vmem),
        scratch_shapes=[
            pltpu.VMEM((ROWS * SC, BS, BS), jnp.float32),
            pltpu.VMEM((NZ, LANES), jnp.int32),
            pltpu.SMEM((NZ, LANES), jnp.int32),
            pltpu.SemaphoreType.DMA,
        ],
        compiler_params=pltpu.CompilerParams(vmem_limit_bytes=24 * 2**20),
        name="consume",
    )(a_all, *msgs)


def body(a_blocks, a_index, a_count, b_blocks, b_rows, b_cols, b_count, c_cols, c_count):
    rep = lax.axis_index("rep")

    def half(value, dim):
        return lax.dynamic_slice_in_dim(value, rep * ROWS, ROWS, dim)

    slots_b = jnp.arange(MB, dtype=jnp.int32)
    own = jnp.stack([jnp.where(slots_b < b_count[0, 0], b_rows[0, 0], -1), b_cols[0, 0]])
    slots_a = jnp.arange(SA, dtype=jnp.int32)
    a_meta = jnp.where(slots_a < a_count[:, :, None], a_index, -2)
    slots_c = jnp.arange(SC, dtype=jnp.int32)
    c_meta = half(jnp.where(slots_c < c_count[:, :, None], c_cols, -1), 0)[:, 0]
    b_own = b_blocks[0, 0]

    b_low = shift_y(b_own[: MB // 2], 1)
    b_high = shift_y(b_own[MB // 2 :], -1)
    other = shift_y(own, 1)
    a_all = lax.all_gather(half(a_blocks, 0).reshape(PAIR, BS, BS), COL)

    a_meta = half(lax.all_gather(a_meta, COL), 1).reshape(NZ, PAIR)
    a_meta = jnp.pad(a_meta, ((0, 0), (0, LANES - PAIR)), constant_values=-2)
    c_meta = jnp.broadcast_to(c_meta.T[:, :, None], (SC, ROWS, PAIR // ROWS)).reshape(SC, PAIR)
    c_meta = jnp.pad(c_meta, ((0, 0), (0, LANES - PAIR)), constant_values=-1).reshape(1, SC * LANES)
    meta = jnp.concatenate([a_meta, jnp.broadcast_to(c_meta, (NZ, SC * LANES))], axis=1)
    meta = spread(meta, "z")

    first = (0, CAP)
    msgs = spread(pack(meta, own, other, b_own, b_low, b_high, *first), "z")
    out, longest = consume(a_all, [msgs], [first])

    def again(_):
        rest = (CAP, PAIR - CAP)
        more = spread(pack(meta, own, other, b_own, b_low, b_high, *rest), "z")
        return consume(a_all, [msgs, more], [first, rest])[0]

    out = lax.cond(longest[0, 0] > CAP, again, lambda done: done, out)
    return out.reshape(ROWS, 1, SC, BS, BS)


def solution(mesh):
    fine = Mesh(mesh.devices.reshape(NZ, NYL, NX, NCORE, NREP), AXES)
    row = ("z", "yl")
    return jax.shard_map(
        body,
        mesh=fine,
        in_specs=tuple(
            P(row, COL, *([None] * (rank - 2))) for rank in (5, 3, 2, 5, 3, 3, 2, 3, 2)
        ),
        out_specs=P(("z", "yl", "rep"), COL, None, None, None),
        check_vma=False,
    )
```

time: 457 us -> 132 us (0.29)
  starting transfers between devices: 219 us -> 11.8 us
  waiting for transfers between devices: 98.6 us -> 5.59 us
  blocking collectives: 0 us -> 80.1 us
  local copies, waits for them, and re-layouts: 61.9 us -> 6.25 us
  matrix products: 42.2 us -> 0 us
  other arithmetic: 12.6 us -> 0.1 us
  Pallas kernels: 0 us -> 11.2 us
  loops' own time: 5.53 us -> 0.01 us
    ppermute x70 -> x3, starting transfers between devices: 219 us -> 3.95 us  [shift_y(): lax.ppermute(value, ('yl', 'rep'), [(y_index(y), y_index((y + steps) % n)...]
    all_to_all x0 -> x1, blocking collectives: none -> 65.8 us  [spread(): return lax.all_to_all(value, axis_name, 0, 0)]
    ppermute x70 -> x3, waiting for transfers between devices: 61.9 us -> 0.01 us  [shift_y(): lax.ppermute(value, ('yl', 'rep'), [(y_index(y), y_index((y + steps) % n)...]
    dot_general x16 -> x0, matrix products: 42.2 us -> none  [the longest x8 29.7 us: accumulate(): jnp.einsum('ias,iaxz->isxz', landing.astype(jnp.float32), products, preci...]
    reduce_scatter x1 -> x0, waiting for transfers between devices: 36.7 us -> none  [body(): lax.psum_scatter(running, 'rep', scatter_dimension=0, tiled=True)]
    gather x32 -> x0, local copies, waits for them, and re-layouts: 18.3 us -> none  [the longest x8 11.8 us: accumulate(): picked = jnp.take(b_blk, where_b, axis=0)]
    all_gather x0 -> x1, blocking collectives: none -> 14.2 us  [body(): a_meta = half(lax.all_gather(a_meta, COL), 1).reshape(NZ, PAIR)]
    dynamic_update_slice x21 -> x0, local copies, waits for them, and re-layouts: 13.6 us -> none  [slab_put(): lax.dynamic_update_index_in_dim(member, update, slab_no, 1)]
  transfers between devices with their start and end apart: 71 -> 5, of which waited for: 9 -> 1; matrix products, arithmetic and copies ran while one was open for 20% -> 2% of each run, Pallas kernels for 0% -> 3%
where the time goes in v1:
time: 132 us; the launch traced here: 130 us
  blocking collectives  80.1 us (61%)
  between operations  14.9 us (11%)
  starting transfers between devices  11.8 us (9%)
  Pallas kernels  11.2 us (8%)
  local copies, waits for them, and re-layouts  6.25 us (5%)
  waiting for transfers between devices  5.59 us (4%)
    all_to_all x1, blocking collectives, spread(): return lax.all_to_all(value, axis_name, 0, 0)  65.8 us
    all_gather x1, blocking collectives, body(): a_meta = half(lax.all_gather(a_meta, COL), 1).reshape(NZ, PAIR)  14.2 us
    all_to_all x1, starting transfers between devices, spread(): return lax.all_to_all(value, axis_name, 0, 0)  7.79 us
    pallas_call x1, Pallas kernels, consume(): pl.pallas_call(functools.partial(consume_kernel, parts), out_shape=(jax.S...  7.35 us
    all_to_all x1, waiting for transfers between devices, spread(): return lax.all_to_all(value, axis_name, 0, 0)  5.56 us
    ppermute x3, starting transfers between devices, shift_y(): lax.ppermute(value, ('yl', 'rep'), [(y_index(y), y_index((y + steps) % n)...  3.95 us
    pallas_call x1, Pallas kernels, pack(): pl.pallas_call(functools.partial(pack_kernel, lo, size), out_shape=jax.Sh...  3.8 us
  transfers between devices with their start and end apart: 5, of which 1 were waited for; matrix products, arithmetic and copies ran while one was open for 2% of the time, Pallas kernels for 3%

profile of v1, /device:TPU:1, one launch (start us, length us, event | category | flops | bytes accessed | tf_op | source)
XLA Modules:
  0.0 129.8 jit_solution(15657954485922789256)
XLA Ops:
  6.5 0.0 copy-start
  6.5 0.0 copy-start.3
  6.5 0.0 copy-start.6
  6.5 0.0 copy-start.7
  6.5 0.0 copy-start.5
  6.5 0.0 copy-start.4
  6.6 0.0 copy-start.9
  6.6 0.0 copy-start.8
  6.6 0.0 all-gather.3.cloned.1.call-start
  6.6 1.2 copy-done
  7.9 0.8 constant_dynamic-slice_fusion.1
  8.7 0.0 all-gather.3.cloned.1.call-update
  8.7 2.3 %slice_bitcast_fusion = (bf16[16,128,128]{2,1,0:T(8,128)(2,1)}, bf16[16,128,128]{2,1,0:T(8,128)(2,1)}) fusion(bf16[1,1,32,128,128]{4,3,2,1,0:T(8,128)(2,1)} %param.14), kind=kLoop, calls=%fused_computation | loop fusion | bytes 2097152 | tf_op jit(solution)/shard_map/slice | solution.py:175
  11.0 3.6 %collective-permute-start.2 = (bf16[16,128,128]{2,1,0:T(8,128)(2,1)}, bf16[16,128,128]{2,1,0:T(8,128)(2,1)S(1)}, u32[]{:S(2)}, u32[]{:S(2)}) collective-permute-start(bf16[16,128,128]{2,1,0:T(8,128)(2,1)} %get-tuple-element.42), channel_id=1, source_target_pairs={{0,17},{16,0},{1,16},{17,1},{2,19},{18,2},{3,18},{19,3},{4,21},{20... | collective-permute-start | bytes 1572872 | tf_op jit(solution)/shard_map/ppermute | solution.py:28
  14.6 0.0 collective-permute-start.1
  14.6 0.0 copy-done.6
  14.6 0.1 copy.17
  14.7 0.0 copy-done.7
  14.7 0.0 copy-done.5
  14.7 0.1 dynamic-slice_bitcast_fusion
  14.8 0.1 broadcast_in_dim.31
  14.8 0.1 reshape.81
  14.9 0.0 copy-done.4
  15.0 0.1 copy.18
  15.0 0.1 compare_select_fusion
  15.1 14.2 %all-gather = s32[64,2,2]{2,1,0:T(2,128)S(1)} all-gather(s32[8,2,2]{2,1,0:T(2,128)S(1)} %compare_select_fusion), channel_id=2, replica_groups=mesh['z'=8,'yl'=2,'x'=4,'core'=2,'rep'=2] {'x','core'}, dimensions={0}, use_global_device_ids=true | all-gather | bytes 1152 | tf_op jit(solution)/shard_map/all_gather | solution.py:179
  29.4 0.1 copy.26
  29.5 0.1 copy.27
  29.6 0.6 all_to_all.13
  30.2 7.8 %all-to-all-start.1 = ((s32[8,1,640]{2,1,0:T(1,128)}), s32[8,1,640]{2,1,0:T(1,128)S(1)}, u32[]{:S(2)}, u32[]{:S(2)}) async-start(s32[8,1,640]{2,1,0:T(1,128)} %all_to_all.13), calls=%async_computation.1 | async-start | bytes 40960 | tf_op jit(solution)/shard_map/all_to_all | solution.py:32
  38.7 0.0 copy-done.9
  38.7 0.0 copy-done.8
  38.7 0.4 collective-permute-start
  39.1 5.6 %all-to-all-done.1 = s32[8,1,640]{2,1,0:T(1,128)S(1)} async-done(((s32[8,1,640]{2,1,0:T(1,128)}), s32[8,1,640]{2,1,0:T(1,128)S(1)}, u32[]{:S(2)}, u32[]{:S(2)}) %all-to-all-start.1) | async-done | bytes 20512 | tf_op jit(solution)/shard_map/all_to_all | solution.py:32
  44.7 0.0 collective-permute-done.other
  44.7 0.0 collective-permute-done.2.b_high
  44.7 0.0 collective-permute-done.1.b_low
  44.7 0.0 copy-done.3
  44.7 3.8 %pack.3 = bf16[8,1296,128]{2,1,0:T(8,128)(2,1)S(1)} custom-call(s32[8,640]{1,0:T(8,128)S(1)} %bitcast.30, s32[2,32]{1,0:T(2,128)S(1)} %pad_add_fusion.own, s32[2,32]{1,0:T(2,128)S(1)} %collective-permute-done.other, bf16[32,128,128]{2,1,0:T(8,128)(2,1)S(1)} %bitcast.27, bf16[16,128,128]{2,1,0:T(8,128)(2,1)S(1)} %collective-permute-done.1.b_low, ...), custom_call_target="tpu_custom_call" | custom-call | tf_op jit(solution)/shard_map/pack/pallas_call | solution.py:87
  48.5 65.8 %all_to_all.21.rest_0_ = bf16[8,1296,128]{2,1,0:T(8,128)(2,1)} all-to-all(bf16[8,1296,128]{2,1,0:T(8,128)(2,1)S(1)} %pack.3), channel_id=1, replica_groups=mesh['z'=8,'yl'=2,'x'=4,'core'=2,'rep'=2] {'z'}, dimensions={0} | all-to-all | bytes 5308416 | tf_op jit(solution)/shard_map/all_to_all | solution.py:32
  114.3 0.0 all-gather.3.cloned.1.call-done.a_all
  114.3 0.0 copy-start.1
  114.3 0.0 copy-start.2
  114.3 7.3 %consume.3 = (bf16[16,128,128]{2,1,0:T(8,128)(2,1)}, s32[8,128]{1,0:T(8,128)S(1)}) custom-call(bf16[8,16,128,128]{3,2,1,0:T(8,128)(2,1)} %all-gather.3.cloned.1.call-done.a_all, bf16[8,1296,128]{2,1,0:T(8,128)(2,1)} %all_to_all.21.rest_0_), custom_call_target="tpu_custom_call" | custom-call | tf_op jit(solution)/shard_map/consume/pallas_call | solution.py:141
  121.7 0.6 slice.19
  122.9 0.0 copy-done.1
  122.9 0.0 copy-done.2
  (9 shorter events, 0.1 us)
Async XLA Ops:
  6.5 1.3 %copy-start = (bf16[8,2,2,128,128]{4,3,2,1,0:T(8,128)(2,1)S(1)}, bf16[8,2,2,128,128]{4,3,2,1,0:T(8,128)(2,1)}, u32[]{:S(2)}) copy-start(bf16[8,2,2,128,128]{4,3,2,1,0:T(8,128)(2,1)} %param.11) | copy-start | bytes 3145732
  6.5 38.1 %copy-start.3 = (bf16[1,1,32,128,128]{4,3,2,1,0:T(8,128)(2,1)S(1)}, bf16[1,1,32,128,128]{4,3,2,1,0:T(8,128)(2,1)}, u32[]{:S(2)}) copy-start(bf16[1,1,32,128,128]{4,3,2,1,0:T(8,128)(2,1)} %param.14) | copy-start | bytes 3145732
  6.5 8.1 %copy-start.6 = (s32[8,2]{0,1:T(2,128)S(1)}, s32[8,2]{0,1:T(2,128)}, u32[]{:S(2)}) copy-start(s32[8,2]{0,1:T(2,128)} %param.13) | copy-start | bytes 196
  6.5 8.1 %copy-start.7 = (s32[8,1]{0,1:T(1,128)S(1)}, s32[8,1]{0,1:T(1,128)}, u32[]{:S(2)}) copy-start(s32[8,1]{0,1:T(1,128)} %param.19) | copy-start | bytes 100
  6.5 8.1 %copy-start.5 = (s32[8,1,4]{0,2,1:T(4,128)S(1)}, s32[8,1,4]{0,2,1:T(4,128)}, u32[]{:S(2)}) copy-start(s32[8,1,4]{0,2,1:T(4,128)} %param.18) | copy-start | bytes 388
  6.5 8.4 %copy-start.4 = (s32[8,2,2]{0,2,1:T(2,128)S(1)}, s32[8,2,2]{0,2,1:T(2,128)}, u32[]{:S(2)}) copy-start(s32[8,2,2]{0,2,1:T(2,128)} %param.12) | copy-start | bytes 388
  6.6 32.1 %copy-start.9 = (s32[1,1,32]{2,1,0:T(1,128)S(1)}, s32[1,1,32]{2,1,0:T(1,128)}, u32[]{:S(2)}) copy-start(s32[1,1,32]{2,1,0:T(1,128)} %param.15) | copy-start | bytes 388
  6.6 32.1 %copy-start.8 = (s32[1,1,32]{2,1,0:T(1,128)S(1)}, s32[1,1,32]{2,1,0:T(1,128)}, u32[]{:S(2)}) copy-start(s32[1,1,32]{2,1,0:T(1,128)} %param.16) | copy-start | bytes 388
  6.6 107.7 %all-gather.3.cloned.1.call-start = ((), (), s32[]{:S(2)}) async-start(), calls=%async_computation.3 | async-start | bytes 4718592 | tf_op jit(solution)/shard_map/all_gather | solution.py:177
  11.0 33.6 %collective-permute-start.2 = (bf16[16,128,128]{2,1,0:T(8,128)(2,1)}, bf16[16,128,128]{2,1,0:T(8,128)(2,1)S(1)}, u32[]{:S(2)}, u32[]{:S(2)}) collective-permute-start(bf16[16,128,128]{2,1,0:T(8,128)(2,1)} %get-tuple-element.42), channel_id=1, source_target_pairs={{0,17},{16,0},{1,16},{17,1},{2,19},{18,2},{3,18},{19,3},{4,21},{20... | collective-permute-start | bytes 1572872 | tf_op jit(solution)/shard_map/ppermute | solution.py:28
  14.6 30.1 %collective-permute-start.1 = (bf16[16,128,128]{2,1,0:T(8,128)(2,1)}, bf16[16,128,128]{2,1,0:T(8,128)(2,1)S(1)}, u32[]{:S(2)}, u32[]{:S(2)}) collective-permute-start(bf16[16,128,128]{2,1,0:T(8,128)(2,1)} %get-tuple-element.43), channel_id=1, source_target_pairs={{0,16},{16,1},{1,17},{17,0},{2,18},{18,3},{3,19},{19,2},{4,20},{20... | collective-permute-start | bytes 1572872 | tf_op jit(solution)/shard_map/ppermute | solution.py:28
  30.2 14.4 %all-to-all-start.1 = ((s32[8,1,640]{2,1,0:T(1,128)}), s32[8,1,640]{2,1,0:T(1,128)S(1)}, u32[]{:S(2)}, u32[]{:S(2)}) async-start(s32[8,1,640]{2,1,0:T(1,128)} %all_to_all.13), calls=%async_computation.1 | async-start | bytes 40960 | tf_op jit(solution)/shard_map/all_to_all | solution.py:32
  38.7 6.0 %collective-permute-start = (s32[2,32]{1,0:T(2,128)S(1)}, s32[2,32]{1,0:T(2,128)S(1)}, u32[]{:S(2)}, u32[]{:S(2)}) collective-permute-start(s32[2,32]{1,0:T(2,128)S(1)} %pad_add_fusion.own), channel_id=1, source_target_pairs={{0,16},{16,1},{1,17},{17,0},{2,18},{18,3},{3,19},{19,2},{4,20},{20... | collective-permute-start | bytes 776 | tf_op jit(solution)/shard_map/ppermute | solution.py:28
  114.3 8.6 %copy-start.1 = (bf16[8,1296,128]{2,1,0:T(8,128)(2,1)S(1)}, bf16[8,1296,128]{2,1,0:T(8,128)(2,1)}, u32[]{:S(2)}) copy-start(bf16[8,1296,128]{2,1,0:T(8,128)(2,1)} %all_to_all.21.rest_0_) | copy-start | bytes 7962628
  114.3 8.6 %copy-start.2 = (bf16[8,16,128,128]{3,2,1,0:T(8,128)(2,1)S(1)}, bf16[8,16,128,128]{3,2,1,0:T(8,128)(2,1)}, u32[]{:S(2)}) copy-start(bf16[8,16,128,128]{3,2,1,0:T(8,128)(2,1)} %all-gather.3.cloned.1.call-done.a_all) | copy-start | bytes 12582916
Sparse Core Ops, SparseCore 0:
  9.3 38.8 all-gather.2

commit v2 on v1

v2 whole, which is shorter than its diff:
```python
import functools

import jax
import jax.numpy as jnp
from jax import lax
from jax.experimental import pallas as pl
from jax.experimental.pallas import tpu as pltpu
from jax.sharding import Mesh
from jax.sharding import PartitionSpec as P

NZ, NYL, NX, NCORE, NREP = 8, 2, 4, 2, 2
AXES = ("z", "yl", "x", "core", "rep")
COL = ("x", "core")
BS, SA, SC, MB = 128, 2, 4, 32
ROWS = 4
PAIR = ROWS * 2 * SA
CAP = 10
HDR = 16
LANES = 128
SHIFTS = (0, 4, 3, -3, 2, -2, 1, -1)
EARLY = 4


def y_index(y):
    return (y % NYL) * NREP + y // NYL


def shift_y(value, steps):
    n = NYL * NREP
    return lax.ppermute(value, ("yl", "rep"), [(y_index(y), y_index((y + steps) % n)) for y in range(n)])


def shift_z(value, steps):
    if steps == 0:
        return value
    return lax.ppermute(value, "z", [(z, (z + steps) % NZ) for z in range(NZ)])


def pack_kernel(lo, size, meta, own, other, b_own, b_low, b_high, *rest):
    outs, (held, codes, scalars, sems) = rest[:NZ], rest[NZ:]
    copies = [
        pltpu.make_async_copy(b_own, held.at[pl.ds(0, MB)], sems.at[0]),
        pltpu.make_async_copy(b_low, held.at[pl.ds(MB, MB // 2)], sems.at[1]),
        pltpu.make_async_copy(b_high, held.at[pl.ds(MB + MB // 2, MB // 2)], sems.at[2]),
    ]
    for copy in copies:
        copy.start()
    yl = lax.axis_index("yl")
    me = lax.axis_index("z")
    col = lax.axis_index("x") * NCORE + lax.axis_index("core")
    lane = lax.broadcasted_iota(jnp.int32, (NZ, LANES), 1)
    is_own = ((lane >> 1) & 1) == yl
    first_half = lax.axis_index("rep") == 0
    wanted = jnp.concatenate([meta[z, pl.ds(me, 1), :] for z in range(NZ)], axis=0)
    wanted = jnp.where(first_half, wanted, pltpu.roll(wanted, LANES - PAIR, 1))
    wanted = jnp.where(lane < PAIR, wanted, -2)
    columns = jnp.concatenate([meta[z, pl.ds(col, 1), :] for z in range(NZ)], axis=0)
    columns = jnp.where(
        first_half,
        pltpu.roll(columns, LANES - 2 * PAIR, 1),
        pltpu.roll(columns, LANES - 2 * PAIR - ROWS * SC, 1),
    )
    moved = {d: pltpu.roll(columns, d % LANES, 1) for d in range(1 - SC, SC)}
    slot = jnp.zeros((NZ, LANES), jnp.int32)
    target = jnp.full((NZ, LANES), -5, jnp.int32)
    for m in range(MB):
        hit = wanted == jnp.where(is_own, own[0, m], other[0, m])
        slot = jnp.where(hit, m, slot)
        target = jnp.where(hit, jnp.where(is_own, own[1, m], other[1, m]), target)
    code = jnp.full((NZ, LANES), -1, jnp.int32)
    for s in range(SC):
        column = moved[-s]
        for o in range(1, SC):
            column = jnp.where((lane & (SC - 1)) == o, moved[o - s], column)
        code = jnp.where(column == target, slot * SC + s, code)
    codes[...] = code
    to_scalars = pltpu.make_async_copy(codes, scalars, sems.at[3])
    to_scalars.start()
    head = jnp.concatenate([code, jnp.full((HDR - NZ, LANES), -1, jnp.int32)], axis=0)
    head = head.astype(jnp.float32).astype(jnp.bfloat16)
    for out in outs:
        out[pl.ds(size * BS, HDR), :] = head
    to_scalars.wait()
    for copy in copies:
        copy.wait()
    for out, shift in zip(outs, SHIFTS):
        z = lax.rem(me + (NZ + shift), NZ)

        def step(t, count, out=out, z=z):
            code = scalars[z, t]
            hit = code >= 0

            @pl.when(hit & (count >= lo) & (count < lo + size))
            def _():
                block = (code >> 2) + jnp.where(((t >> 1) & 1) == yl, 0, MB)
                out[pl.ds(pl.multiple_of((count - lo) * BS, BS), BS), :] = held[block]

            return count + hit.astype(jnp.int32)

        lax.fori_loop(0, PAIR, step, jnp.int32(0))


def pack(meta, own, other, b_own, b_low, b_high, lo, size):
    smem, vmem, hbm = (pl.BlockSpec(memory_space=m) for m in (pltpu.SMEM, pltpu.VMEM, pl.ANY))
    return pl.pallas_call(
        functools.partial(pack_kernel, lo, size),
        out_shape=[jax.ShapeDtypeStruct((size * BS + HDR, BS), jnp.bfloat16)] * NZ,
        in_specs=[vmem, smem, smem, hbm, hbm, hbm],
        out_specs=[vmem] * NZ,
        scratch_shapes=[
            pltpu.VMEM((2 * MB, BS, BS), jnp.bfloat16),
            pltpu.VMEM((NZ, LANES), jnp.int32),
            pltpu.SMEM((NZ, LANES), jnp.int32),
            pltpu.SemaphoreType.DMA((4,)),
        ],
        compiler_params=pltpu.CompilerParams(vmem_limit_bytes=24 * 2**20),
        name="pack",
    )(meta, own, other, b_own, b_low, b_high)


def consume_kernel(shifts, parts, final, a_all, total_in, longest_in, *rest):
    count_msgs = len(shifts) * len(parts)
    msgs, (out, longest, total, codes, scalars, sem) = rest[:count_msgs], rest[count_msgs:]
    me = lax.axis_index("z")
    row = lax.broadcasted_iota(jnp.int32, (HDR, LANES), 0)
    most = jnp.zeros((HDR, 1), jnp.int32)
    for n in range(len(shifts)):
        head = msgs[n * len(parts)][pl.ds(parts[0][1] * BS, HDR), :].astype(jnp.float32).astype(jnp.int32)
        codes[pl.ds(n, 1), :] = jnp.sum(jnp.where(row == me, head, 0), axis=0, keepdims=True)
        most = jnp.maximum(most, jnp.sum((head >= 0).astype(jnp.int32), axis=1, keepdims=True))
    to_scalars = pltpu.make_async_copy(codes, scalars, sem)
    to_scalars.start()
    most = jnp.broadcast_to(jnp.max(most, axis=0, keepdims=True), longest.shape)
    longest[...] = jnp.maximum(most, longest_in[...])
    total[...] = total_in[...]
    to_scalars.wait()
    for n, shift in enumerate(shifts):
        source = lax.rem(me + (NZ - shift), NZ)

        def step(t, count, n=n, source=source):
            code = scalars[n, t]
            hit = code >= 0
            place = (t >> 2) * SC + (code & 3)
            for part, (lo, size) in enumerate(parts):

                @pl.when(hit & (count >= lo) & (count < lo + size))
                def _(lo=lo, msg=msgs[n * len(parts) + part]):
                    block = msg[pl.ds(pl.multiple_of((count - lo) * BS, BS), BS), :]
                    total[place] += jnp.dot(a_all[source, t], block, preferred_element_type=jnp.float32)

            return count + hit.astype(jnp.int32)

        lax.fori_loop(0, PAIR, step, jnp.int32(0))
    if final:
        out[...] = total[...].astype(out.dtype)
    else:
        out[...] = total[...]


def consume(a_all, total, longest, shifts, parts, msgs, final):
    vmem = pl.BlockSpec(memory_space=pltpu.VMEM)
    shape = (ROWS * SC, BS, BS)
    return pl.pallas_call(
        functools.partial(consume_kernel, shifts, parts, final),
        out_shape=(
            jax.ShapeDtypeStruct(shape, jnp.bfloat16 if final else jnp.float32),
            jax.ShapeDtypeStruct((8, LANES), jnp.int32),
        ),
        in_specs=[vmem] * (3 + len(msgs)),
        out_specs=(vmem, vmem),
        scratch_shapes=[
            pltpu.VMEM(shape, jnp.float32),
            pltpu.VMEM((NZ, LANES), jnp.int32),
            pltpu.SMEM((NZ, LANES), jnp.int32),
            pltpu.SemaphoreType.DMA,
        ],
        compiler_params=pltpu.CompilerParams(vmem_limit_bytes=24 * 2**20),
        cost_estimate=pl.CostEstimate(flops=2 * BS**3 * 40, bytes_accessed=8 * 2**20, transcendentals=0),
        name="consume",
    )(a_all, total, longest, *msgs)


def body(a_blocks, a_index, a_count, b_blocks, b_rows, b_cols, b_count, c_cols, c_count):
    rep = lax.axis_index("rep")

    slots_b = jnp.arange(MB, dtype=jnp.int32)
    own = jnp.stack([jnp.where(slots_b < b_count[0, 0], b_rows[0, 0], -1), b_cols[0, 0]])
    slots_a = jnp.arange(SA, dtype=jnp.int32)
    a_meta = jnp.where(slots_a < a_count[:, :, None], a_index, -2)
    slots_c = jnp.arange(SC, dtype=jnp.int32)
    c_meta = jnp.where(slots_c < c_count[:, :, None], c_cols, -1)
    b_own = b_blocks[0, 0]

    other = shift_y(own, 1)
    b_low = shift_y(b_own[: MB // 2], 1)
    b_high = shift_y(b_own[MB // 2 :], -1)

    meta = jnp.concatenate([a_meta.reshape(2 * PAIR), c_meta.reshape(2 * ROWS * SC)])
    meta = jnp.pad(meta, (0, LANES - meta.shape[0]))
    meta = jnp.broadcast_to(meta[None, :], (NZ * NX * NCORE, LANES))
    meta = lax.all_to_all(meta, ("z", "x", "core"), 0, 0).reshape(NZ, NX * NCORE, LANES)

    start = rep * ROWS + jnp.minimum(meta[0, 0, 0] + 2, 0)
    a_all = lax.dynamic_slice_in_dim(a_blocks, start, ROWS, 0).reshape(PAIR, BS, BS)
    a_all = lax.all_gather(a_all, COL)

    def send(lo, size):
        outs = pack(meta, own, other, b_own, b_low, b_high, lo, size)
        return [shift_z(out, shift) for out, shift in zip(outs, SHIFTS)]

    first = (0, CAP)
    msgs = send(*first)
    total = jnp.zeros((ROWS * SC, BS, BS), jnp.float32)
    longest = jnp.zeros((8, LANES), jnp.int32)
    total, longest = consume(a_all, total, longest, SHIFTS[:EARLY], [first], msgs[:EARLY], False)
    out, longest = consume(a_all, total, longest, SHIFTS[EARLY:], [first], msgs[EARLY:], True)

    def again(_):
        rest = (CAP, PAIR - CAP)
        both = [msg for pair in zip(msgs, send(*rest)) for msg in pair]
        zero = jnp.zeros((ROWS * SC, BS, BS), jnp.float32)
        return consume(a_all, zero, longest, SHIFTS, [first, rest], both, True)[0]

    out = lax.cond(longest[0, 0] > CAP, again, lambda done: done, out)
    return out.reshape(ROWS, 1, SC, BS, BS)


def solution(mesh):
    fine = Mesh(mesh.devices.reshape(NZ, NYL, NX, NCORE, NREP), AXES)
    row = ("z", "yl")
    return jax.shard_map(
        body,
        mesh=fine,
        in_specs=tuple(
            P(row, COL, *([None] * (rank - 2))) for rank in (5, 3, 2, 5, 3, 3, 2, 3, 2)
        ),
        out_specs=P(("z", "yl", "rep"), COL, None, None, None),
        check_vma=False,
    )
```

time: 132 us -> 131 us (level); the launches traced: 130 us -> 130 us
  blocking collectives: 80.1 us -> 0 us
  waiting for transfers between devices: 5.59 us -> 61.2 us
  starting transfers between devices: 11.8 us -> 32.7 us
  other arithmetic: 0.1 us -> 2.94 us
  Pallas kernels: 11.2 us -> 13.5 us
  local copies, waits for them, and re-layouts: 6.25 us -> 4.31 us
    all_to_all x1 -> x0, blocking collectives: 65.8 us -> none  [spread(): return lax.all_to_all(value, axis_name, 0, 0)]
    ppermute x0 -> x7, waiting for transfers between devices: none -> 40.1 us  [shift_z(): return lax.ppermute(value, 'z', [(z, (z + steps) % NZ) for z in range(NZ)])]
    ppermute x0 -> x7, starting transfers between devices: none -> 16.8 us  [shift_z(): return lax.ppermute(value, 'z', [(z, (z + steps) % NZ) for z in range(NZ)])]
    all_gather x1 -> x0, blocking collectives: 14.2 us -> none  [body(): a_meta = half(lax.all_gather(a_meta, COL), 1).reshape(NZ, PAIR)]
    ppermute x3, waiting for transfers between devices: 0.01 us -> 11.8 us  [shift_y(): lax.ppermute(value, ('yl', 'rep'), [(y_index(y), y_index((y + steps) % n)...]
    all_to_all x1, starting transfers between devices: 7.79 us -> 13 us  [body(): lax.all_to_all(meta, ('z', 'x', 'core'), 0, 0)]
    all_to_all x1, waiting for transfers between devices: 5.56 us -> 9.25 us  [body(): lax.all_to_all(meta, ('z', 'x', 'core'), 0, 0)]
    pallas_call x2 -> x3, Pallas kernels: 11.2 us -> 13.5 us  [the longest x2 8.76 us: consume(): pl.pallas_call(functools.partial(consume_kernel, shifts, parts, final), o...]
  transfers between devices with their start and end apart: 5 -> 12, of which waited for: 1 -> 7; matrix products, arithmetic and copies ran while one was open for 2% -> 2% of each run, Pallas kernels for 3% -> 7%
where the time goes in v2:
time: 131 us; the launch traced here: 130 us
  waiting for transfers between devices  61.2 us (47%)
  starting transfers between devices  32.7 us (25%)
  between operations  15.6 us (12%)
  Pallas kernels  13.5 us (10%)
  local copies, waits for them, and re-layouts  4.31 us (3%)
  other arithmetic  2.94 us (2%)
    ppermute x7, waiting for transfers between devices, shift_z(): return lax.ppermute(value, 'z', [(z, (z + steps) % NZ) for z in range(NZ)])  40.1 us
    ppermute x7, starting transfers between devices, shift_z(): return lax.ppermute(value, 'z', [(z, (z + steps) % NZ) for z in range(NZ)])  16.8 us
    all_to_all x1, starting transfers between devices, body(): lax.all_to_all(meta, ('z', 'x', 'core'), 0, 0)  13 us
    ppermute x3, waiting for transfers between devices, shift_y(): lax.ppermute(value, ('yl', 'rep'), [(y_index(y), y_index((y + steps) % n)...  11.8 us
    all_to_all x1, waiting for transfers between devices, body(): lax.all_to_all(meta, ('z', 'x', 'core'), 0, 0)  9.25 us
    pallas_call x2, Pallas kernels, consume(): pl.pallas_call(functools.partial(consume_kernel, shifts, parts, final), o...  8.76 us
    pallas_call x1, Pallas kernels, pack(): pl.pallas_call(functools.partial(pack_kernel, lo, size), out_shape=[jax.S...  4.69 us
    ppermute x3, starting transfers between devices, shift_y(): lax.ppermute(value, ('yl', 'rep'), [(y_index(y), y_index((y + steps) % n)...  2.84 us
  transfers between devices with their start and end apart: 12, of which 7 were waited for; matrix products, arithmetic and copies ran while one was open for 2% of the time, Pallas kernels for 7%

profile of v2, /device:TPU:1, one launch (start us, length us, event | category | flops | bytes accessed | tf_op | source)
XLA Modules:
  0.0 130.4 jit_solution(7821470262369701758)
XLA Ops:
  6.5 0.8 fusion
  7.4 0.1 copy.19
  7.5 0.1 reshape.90
  7.5 0.7 compare_select_fusion
  8.2 0.1 copy.18
  8.3 0.1 reshape.89
  8.4 0.1 pad_add_fusion.1
  8.5 0.6 broadcast_in_dim.27
  9.2 13.0 %all-to-all-start = ((s32[64,1,128]{2,1,0:T(1,128)}), s32[64,1,128]{2,1,0:T(1,128)S(1)}, u32[]{:S(2)}, u32[]{:S(2)}) async-start(s32[64,1,128]{2,1,0:T(1,128)} %broadcast_in_dim.27), calls=%async_computation | async-start | bytes 65536 | tf_op jit(solution)/shard_map/all_to_all | solution.py:201
  22.2 0.0 all-gather.2.cloned.1.call-start
  22.2 9.2 %all-to-all-done = s32[64,1,128]{2,1,0:T(1,128)S(1)} async-done(((s32[64,1,128]{2,1,0:T(1,128)}), s32[64,1,128]{2,1,0:T(1,128)S(1)}, u32[]{:S(2)}, u32[]{:S(2)}) %all-to-all-start) | async-done | bytes 32800 | tf_op jit(solution)/shard_map/all_to_all | solution.py:201
  31.5 0.5 slice.24
  32.6 0.0 copy-done
  32.6 0.8 constant_dynamic-slice_fusion
  33.5 0.0 all-gather.2.cloned.1.call-update
  33.5 1.3 slice_bitcast_fusion
  34.8 2.8 %collective-permute-start.9 = (bf16[16,128,128]{2,1,0:T(8,128)(2,1)S(1)}, bf16[16,128,128]{2,1,0:T(8,128)(2,1)S(1)}, u32[]{:S(2)}, u32[]{:S(2)}) collective-permute-start(bf16[16,128,128]{2,1,0:T(8,128)(2,1)S(1)} %get-tuple-element.94), channel_id=1, source_target_pairs={{0,17},{16,0},{1,16},{17,1},{2,19},{18,2},{3,18},{19,3},{4,21},{20... | collective-permute-start | bytes 1572872 | tf_op jit(solution)/shard_map/ppermute | solution.py:30
  37.6 0.0 collective-permute-start.8
  38.3 0.7 compare_select_fusion.1
  38.9 0.7 pad_add_fusion.own
  39.6 0.0 collective-permute-start.7
  39.6 11.8 %collective-permute-done.7.other = s32[2,32]{1,0:T(2,128)S(1)} collective-permute-done((s32[2,32]{1,0:T(2,128)S(1)}, s32[2,32]{1,0:T(2,128)S(1)}, u32[]{:S(2)}, u32[]{:S(2)}) %collective-permute-start.7) | collective-permute-done | bytes 288 | tf_op jit(solution)/shard_map/ppermute | solution.py:30
  51.4 0.0 collective-permute-done.9.b_high
  51.4 0.0 collective-permute-done.8.b_low
  51.4 0.0 copy-start.5
  51.4 0.0 copy-done.2
  51.4 4.7 %pack.3 = (bf16[1296,128]{1,0:T(8,128)(2,1)}, bf16[1296,128]{1,0:T(8,128)(2,1)S(1)}, bf16[1296,128]{1,0:T(8,128)(2,1)S(1)}, bf16[1296,128]{1,0:T(8,128)(2,1)S(1)...) custom-call(s32[8,8,128]{2,1,0:T(8,128)S(1)} %bitcast.24, ...), custom_call_target="tpu_custom_call" | custom-call | tf_op jit(solution)/shard_map/pack/pallas_call | solution.py:105
  56.1 0.1 collective-permute-start.10
  56.3 3.2 %collective-permute-start.11 = (bf16[1296,128]{1,0:T(8,128)(2,1)S(1)}, bf16[1296,128]{1,0:T(8,128)(2,1)S(1)}, u32[]{:S(2)}, u32[]{:S(2)}) collective-permute-start(bf16[1296,128]{1,0:T(8,128)(2,1)S(1)} %get-tuple-element.82), channel_id=1, source_target_pairs={{0,96},{32,128},{64,160},{96,192},{128,224},{160,0},{192,32},{224,... | collective-permute-start | bytes 995336 | tf_op jit(solution)/shard_map/ppermute | solution.py:36
  59.4 1.3 %collective-permute-start.12 = (bf16[1296,128]{1,0:T(8,128)(2,1)S(1)}, bf16[1296,128]{1,0:T(8,128)(2,1)}, u32[]{:S(2)}, u32[]{:S(2)}) collective-permute-start(bf16[1296,128]{1,0:T(8,128)(2,1)S(1)} %get-tuple-element.83), channel_id=1, source_target_pairs={{0,160},{32,192},{64,224},{96,0},{128,32},{160,64},{192,96},{224,1... | collective-permute-start | bytes 995336 | tf_op jit(solution)/shard_map/ppermute | solution.py:36
  60.8 2.2 %collective-permute-start.13 = (bf16[1296,128]{1,0:T(8,128)(2,1)S(1)}, bf16[1296,128]{1,0:T(8,128)(2,1)}, u32[]{:S(2)}, u32[]{:S(2)}) collective-permute-start(bf16[1296,128]{1,0:T(8,128)(2,1)S(1)} %get-tuple-element.86), channel_id=1, source_target_pairs={{0,64},{32,96},{64,128},{96,160},{128,192},{160,224},{192,0},{224,... | collective-permute-start | bytes 995336 | tf_op jit(solution)/shard_map/ppermute | solution.py:36
  63.0 1.4 %collective-permute-start.14 = (bf16[1296,128]{1,0:T(8,128)(2,1)S(1)}, bf16[1296,128]{1,0:T(8,128)(2,1)}, u32[]{:S(2)}, u32[]{:S(2)}) collective-permute-start(bf16[1296,128]{1,0:T(8,128)(2,1)S(1)} %get-tuple-element.87), channel_id=1, source_target_pairs={{0,192},{32,224},{64,0},{96,32},{128,64},{160,96},{192,128},{224,1... | collective-permute-start | bytes 995336 | tf_op jit(solution)/shard_map/ppermute | solution.py:36
  64.4 5.3 %collective-permute-done.10.rest_1_ = bf16[1296,128]{1,0:T(8,128)(2,1)S(1)} collective-permute-done((bf16[1296,128]{1,0:T(8,128)(2,1)S(1)}, bf16[1296,128]{1,0:T(8,128)(2,1)S(1)}, u32[]{:S(2)}, u32[]{:S(2)}) %collective-permute-start.10) | collective-permute-done | bytes 331808 | tf_op jit(solution)/shard_map/ppermute | solution.py:36
  69.7 5.7 %collective-permute-start.15 = (bf16[1296,128]{1,0:T(8,128)(2,1)S(1)}, bf16[1296,128]{1,0:T(8,128)(2,1)}, u32[]{:S(2)}, u32[]{:S(2)}) collective-permute-start(bf16[1296,128]{1,0:T(8,128)(2,1)S(1)} %get-tuple-element.88), channel_id=1, source_target_pairs={{0,32},{32,64},{64,96},{96,128},{128,160},{160,192},{192,224},{224... | collective-permute-start | bytes 995336 | tf_op jit(solution)/shard_map/ppermute | solution.py:36
  75.4 18.8 %collective-permute-done.11.rest_2_ = bf16[1296,128]{1,0:T(8,128)(2,1)S(1)} collective-permute-done((bf16[1296,128]{1,0:T(8,128)(2,1)S(1)}, bf16[1296,128]{1,0:T(8,128)(2,1)S(1)}, u32[]{:S(2)}, u32[]{:S(2)}) %collective-permute-start.11) | collective-permute-done | bytes 331808 | tf_op jit(solution)/shard_map/ppermute | solution.py:36
  94.1 2.9 %collective-permute-start.16 = (bf16[1296,128]{1,0:T(8,128)(2,1)S(1)}, bf16[1296,128]{1,0:T(8,128)(2,1)}, u32[]{:S(2)}, u32[]{:S(2)}) collective-permute-start(bf16[1296,128]{1,0:T(8,128)(2,1)S(1)} %get-tuple-element.89), channel_id=1, source_target_pairs={{0,224},{32,0},{64,32},{96,64},{128,96},{160,128},{192,160},{224,1... | collective-permute-start | bytes 995336 | tf_op jit(solution)/shard_map/ppermute | solution.py:36
  97.0 0.0 copy-done.3
  97.0 0.0 collective-permute-done.12.rest_3_
  97.0 0.0 all-gather.2.cloned.1.call-done.a_all
  97.1 0.1 broadcast_3_total_in.2.total_in
  97.2 4.7 %consume.4 = (f32[16,128,128]{2,1,0:T(8,128)S(1)}, s32[8,128]{1,0:T(8,128)S(1)}) custom-call(bf16[8,16,128,128]{3,2,1,0:T(8,128)(2,1)} %all-gather.2.cloned.1.call-done.a_all, f32[16,128,128]{2,1,0:T(8,128)S(1)} %broadcast_3_total_in.2.total_in, s32[8,128]{1,0:T(8,128)S(1)} %broadcast_in_dim.28.longest_in, bf16[1296,128]{1,0:T(8,128)(2,1)} %get-tuple-element.80.rest_0_, ...), custom_call_target="tpu_custom_call" | custom-call | flops 167772160 | bytes 8388608 | tf_op jit(solution)/shard_map/consume/pallas_call | solution.py:163
  102.0 4.0 %collective-permute-done.13.rest_0_ = bf16[1296,128]{1,0:T(8,128)(2,1)} collective-permute-done((bf16[1296,128]{1,0:T(8,128)(2,1)S(1)}, bf16[1296,128]{1,0:T(8,128)(2,1)}, u32[]{:S(2)}, u32[]{:S(2)}) %collective-permute-start.13) | collective-permute-done | bytes 331808 | tf_op jit(solution)/shard_map/ppermute | solution.py:36
  105.9 4.6 %collective-permute-done.14.rest_1_ = bf16[1296,128]{1,0:T(8,128)(2,1)} collective-permute-done((bf16[1296,128]{1,0:T(8,128)(2,1)S(1)}, bf16[1296,128]{1,0:T(8,128)(2,1)}, u32[]{:S(2)}, u32[]{:S(2)}) %collective-permute-start.14) | collective-permute-done | bytes 331808 | tf_op jit(solution)/shard_map/ppermute | solution.py:36
  110.6 7.4 %collective-permute-done.15.rest_2_ = bf16[1296,128]{1,0:T(8,128)(2,1)} collective-permute-done((bf16[1296,128]{1,0:T(8,128)(2,1)S(1)}, bf16[1296,128]{1,0:T(8,128)(2,1)}, u32[]{:S(2)}, u32[]{:S(2)}) %collective-permute-start.15) | collective-permute-done | bytes 331808 | tf_op jit(solution)/shard_map/ppermute | solution.py:36
  118.0 0.0 collective-permute-done.16.rest_3_
  118.0 4.0 %consume.5 = (bf16[16,128,128]{2,1,0:T(8,128)(2,1)}, s32[8,128]{1,0:T(8,128)S(1)}) custom-call(bf16[8,16,128,128]{3,2,1,0:T(8,128)(2,1)S(1)} %copy-done.1, f32[16,128,128]{2,1,0:T(8,128)S(1)} %get-tuple-element.84.total_in, s32[8,128]{1,0:T(8,128)S(1)} %get-tuple-element.85.longest_in, bf16[1296,128]{1,0:T(8,128)(2,1)} %collective-permute-done.13.rest_0_, ...), custom_call_target="tpu_custom_call" | custom-call | flops 167772160 | bytes 8388608 | tf_op jit(solution)/shard_map/consume/pallas_call | solution.py:163
  122.1 0.5 slice.23
  123.3 0.2 conditional.1
  (22 shorter events, 0.0 us)
Async XLA Ops:
  6.5 26.1 %copy-start = (bf16[8,2,2,128,128]{4,3,2,1,0:T(8,128)(2,1)S(1)}, bf16[8,2,2,128,128]{4,3,2,1,0:T(8,128)(2,1)}, u32[]{:S(2)}) copy-start(bf16[8,2,2,128,128]{4,3,2,1,0:T(8,128)(2,1)} %param.11) | copy-start | bytes 3145732
  6.5 44.9 %copy-start.2 = (bf16[1,1,32,128,128]{4,3,2,1,0:T(8,128)(2,1)S(1)}, bf16[1,1,32,128,128]{4,3,2,1,0:T(8,128)(2,1)}, u32[]{:S(2)}) copy-start(bf16[1,1,32,128,128]{4,3,2,1,0:T(8,128)(2,1)} %param.14) | copy-start | bytes 3145732
  9.2 22.3 %all-to-all-start = ((s32[64,1,128]{2,1,0:T(1,128)}), s32[64,1,128]{2,1,0:T(1,128)S(1)}, u32[]{:S(2)}, u32[]{:S(2)}) async-start(s32[64,1,128]{2,1,0:T(1,128)} %broadcast_in_dim.27), calls=%async_computation | async-start | bytes 65536 | tf_op jit(solution)/shard_map/all_to_all | solution.py:201
  22.2 74.9 %all-gather.2.cloned.1.call-start = ((), (), s32[]{:S(2)}) async-start(), calls=%async_computation.1 | async-start | bytes 4718592 | tf_op jit(solution)/shard_map/all_gather | solution.py:205
  34.8 16.6 %collective-permute-start.9 = (bf16[16,128,128]{2,1,0:T(8,128)(2,1)S(1)}, bf16[16,128,128]{2,1,0:T(8,128)(2,1)S(1)}, u32[]{:S(2)}, u32[]{:S(2)}) collective-permute-start(bf16[16,128,128]{2,1,0:T(8,128)(2,1)S(1)} %get-tuple-element.94), channel_id=1, source_target_pairs={{0,17},{16,0},{1,16},{17,1},{2,19},{18,2},{3,18},{19,3},{4,21},{20... | collective-permute-start | bytes 1572872 | tf_op jit(solution)/shard_map/ppermute | solution.py:30
  37.6 13.8 %collective-permute-start.8 = (bf16[16,128,128]{2,1,0:T(8,128)(2,1)S(1)}, bf16[16,128,128]{2,1,0:T(8,128)(2,1)S(1)}, u32[]{:S(2)}, u32[]{:S(2)}) collective-permute-start(bf16[16,128,128]{2,1,0:T(8,128)(2,1)S(1)} %get-tuple-element.95), channel_id=1, source_target_pairs={{0,16},{16,1},{1,17},{17,0},{2,18},{18,3},{3,19},{19,2},{4,20},{20... | collective-permute-start | bytes 1572872 | tf_op jit(solution)/shard_map/ppermute | solution.py:30
  39.6 11.8 %collective-permute-start.7 = (s32[2,32]{1,0:T(2,128)S(1)}, s32[2,32]{1,0:T(2,128)S(1)}, u32[]{:S(2)}, u32[]{:S(2)}) collective-permute-start(s32[2,32]{1,0:T(2,128)S(1)} %pad_add_fusion.own), channel_id=1, source_target_pairs={{0,16},{16,1},{1,17},{17,0},{2,18},{18,3},{3,19},{19,2},{4,20},{20... | collective-permute-start | bytes 776 | tf_op jit(solution)/shard_map/ppermute | solution.py:30
  51.4 45.6 %copy-start.3 = (bf16[16,128,128]{2,1,0:T(8,128)(2,1)}, bf16[16,128,128]{2,1,0:T(8,128)(2,1)S(1)}, u32[]{:S(2)}) copy-start(bf16[16,128,128]{2,1,0:T(8,128)(2,1)S(1)} %collective-permute-done.9.b_high) | copy-start | bytes 1572868
  51.4 45.6 %copy-start.5 = (bf16[16,128,128]{2,1,0:T(8,128)(2,1)}, bf16[16,128,128]{2,1,0:T(8,128)(2,1)S(1)}, u32[]{:S(2)}) copy-start(bf16[16,128,128]{2,1,0:T(8,128)(2,1)S(1)} %collective-permute-done.8.b_low) | copy-start | bytes 1572868
  56.1 13.5 %collective-permute-start.10 = (bf16[1296,128]{1,0:T(8,128)(2,1)S(1)}, bf16[1296,128]{1,0:T(8,128)(2,1)S(1)}, u32[]{:S(2)}, u32[]{:S(2)}) collective-permute-start(bf16[1296,128]{1,0:T(8,128)(2,1)S(1)} %get-tuple-element.81), channel_id=1, source_target_pairs={{0,128},{32,160},{64,192},{96,224},{128,0},{160,32},{192,64},{224,... | collective-permute-start | bytes 995336 | tf_op jit(solution)/shard_map/ppermute | solution.py:36
  56.3 37.8 %collective-permute-start.11 = (bf16[1296,128]{1,0:T(8,128)(2,1)S(1)}, bf16[1296,128]{1,0:T(8,128)(2,1)S(1)}, u32[]{:S(2)}, u32[]{:S(2)}) collective-permute-start(bf16[1296,128]{1,0:T(8,128)(2,1)S(1)} %get-tuple-element.82), channel_id=1, source_target_pairs={{0,96},{32,128},{64,160},{96,192},{128,224},{160,0},{192,32},{224,... | collective-permute-start | bytes 995336 | tf_op jit(solution)/shard_map/ppermute | solution.py:36
  59.4 37.6 %collective-permute-start.12 = (bf16[1296,128]{1,0:T(8,128)(2,1)S(1)}, bf16[1296,128]{1,0:T(8,128)(2,1)}, u32[]{:S(2)}, u32[]{:S(2)}) collective-permute-start(bf16[1296,128]{1,0:T(8,128)(2,1)S(1)} %get-tuple-element.83), channel_id=1, source_target_pairs={{0,160},{32,192},{64,224},{96,0},{128,32},{160,64},{192,96},{224,1... | collective-permute-start | bytes 995336 | tf_op jit(solution)/shard_map/ppermute | solution.py:36
  60.8 45.2 %collective-permute-start.13 = (bf16[1296,128]{1,0:T(8,128)(2,1)S(1)}, bf16[1296,128]{1,0:T(8,128)(2,1)}, u32[]{:S(2)}, u32[]{:S(2)}) collective-permute-start(bf16[1296,128]{1,0:T(8,128)(2,1)S(1)} %get-tuple-element.86), channel_id=1, source_target_pairs={{0,64},{32,96},{64,128},{96,160},{128,192},{160,224},{192,0},{224,... | collective-permute-start | bytes 995336 | tf_op jit(solution)/shard_map/ppermute | solution.py:36
  63.0 47.6 %collective-permute-start.14 = (bf16[1296,128]{1,0:T(8,128)(2,1)S(1)}, bf16[1296,128]{1,0:T(8,128)(2,1)}, u32[]{:S(2)}, u32[]{:S(2)}) collective-permute-start(bf16[1296,128]{1,0:T(8,128)(2,1)S(1)} %get-tuple-element.87), channel_id=1, source_target_pairs={{0,192},{32,224},{64,0},{96,32},{128,64},{160,96},{192,128},{224,1... | collective-permute-start | bytes 995336 | tf_op jit(solution)/shard_map/ppermute | solution.py:36
  69.7 27.3 %copy-start.8 = (bf16[1296,128]{1,0:T(8,128)(2,1)}, bf16[1296,128]{1,0:T(8,128)(2,1)S(1)}, u32[]{:S(2)}) copy-start(bf16[1296,128]{1,0:T(8,128)(2,1)S(1)} %collective-permute-done.10.rest_1_) | copy-start | bytes 995332
  69.7 48.3 %collective-permute-start.15 = (bf16[1296,128]{1,0:T(8,128)(2,1)S(1)}, bf16[1296,128]{1,0:T(8,128)(2,1)}, u32[]{:S(2)}, u32[]{:S(2)}) collective-permute-start(bf16[1296,128]{1,0:T(8,128)(2,1)S(1)} %get-tuple-element.88), channel_id=1, source_target_pairs={{0,32},{32,64},{64,96},{96,128},{128,160},{160,192},{192,224},{224... | collective-permute-start | bytes 995336 | tf_op jit(solution)/shard_map/ppermute | solution.py:36
  94.1 2.9 %copy-start.10 = (bf16[1296,128]{1,0:T(8,128)(2,1)}, bf16[1296,128]{1,0:T(8,128)(2,1)S(1)}, u32[]{:S(2)}) copy-start(bf16[1296,128]{1,0:T(8,128)(2,1)S(1)} %collective-permute-done.11.rest_2_) | copy-start | bytes 995332
  94.1 23.9 %collective-permute-start.16 = (bf16[1296,128]{1,0:T(8,128)(2,1)S(1)}, bf16[1296,128]{1,0:T(8,128)(2,1)}, u32[]{:S(2)}, u32[]{:S(2)}) collective-permute-start(bf16[1296,128]{1,0:T(8,128)(2,1)S(1)} %get-tuple-element.89), channel_id=1, source_target_pairs={{0,224},{32,0},{64,32},{96,64},{128,96},{160,128},{192,160},{224,1... | collective-permute-start | bytes 995336 | tf_op jit(solution)/shard_map/ppermute | solution.py:36
  97.1 21.0 %copy-start.1 = (bf16[8,16,128,128]{3,2,1,0:T(8,128)(2,1)S(1)}, bf16[8,16,128,128]{3,2,1,0:T(8,128)(2,1)}, u32[]{:S(2)}) copy-start(bf16[8,16,128,128]{3,2,1,0:T(8,128)(2,1)} %all-gather.2.cloned.1.call-done.a_all) | copy-start | bytes 12582916
  101.9 21.3 %copy-start.4 = (bf16[16,128,128]{2,1,0:T(8,128)(2,1)S(1)}, bf16[16,128,128]{2,1,0:T(8,128)(2,1)}, u32[]{:S(2)}) copy-start(bf16[16,128,128]{2,1,0:T(8,128)(2,1)} %copy-done.3) | copy-start | bytes 1572868
  101.9 21.3 %copy-start.6 = (bf16[16,128,128]{2,1,0:T(8,128)(2,1)S(1)}, bf16[16,128,128]{2,1,0:T(8,128)(2,1)}, u32[]{:S(2)}) copy-start(bf16[16,128,128]{2,1,0:T(8,128)(2,1)} %copy-done.5) | copy-start | bytes 1572868
  101.9 21.3 %copy-start.7 = (bf16[1296,128]{1,0:T(8,128)(2,1)S(1)}, bf16[1296,128]{1,0:T(8,128)(2,1)}, u32[]{:S(2)}) copy-start(bf16[1296,128]{1,0:T(8,128)(2,1)} %get-tuple-element.80.rest_0_) | copy-start | bytes 995332
  102.0 21.3 %copy-start.9 = (bf16[1296,128]{1,0:T(8,128)(2,1)S(1)}, bf16[1296,128]{1,0:T(8,128)(2,1)}, u32[]{:S(2)}) copy-start(bf16[1296,128]{1,0:T(8,128)(2,1)} %copy-done.8) | copy-start | bytes 995332
  102.0 21.3 %copy-start.11 = (bf16[1296,128]{1,0:T(8,128)(2,1)S(1)}, bf16[1296,128]{1,0:T(8,128)(2,1)}, u32[]{:S(2)}) copy-start(bf16[1296,128]{1,0:T(8,128)(2,1)} %copy-done.10) | copy-start | bytes 995332
Sparse Core Ops, SparseCore 0:
  33.6 29.7 all-gather.1

commit v3 on v2

--- a/solution.py
+++ b/solution.py
@@ -191,6 +191,9 @@
     c_meta = jnp.where(slots_c < c_count[:, :, None], c_cols, -1)
     b_own = b_blocks[0, 0]
 
+    a_all = lax.dynamic_slice_in_dim(a_blocks, rep * ROWS, ROWS, 0).reshape(PAIR, BS, BS)
+    a_all = lax.all_gather(a_all, COL)
+
     other = shift_y(own, 1)
     b_low = shift_y(b_own[: MB // 2], 1)
     b_high = shift_y(b_own[MB // 2 :], -1)
@@ -199,10 +202,6 @@
     meta = jnp.pad(meta, (0, LANES - meta.shape[0]))
     meta = jnp.broadcast_to(meta[None, :], (NZ * NX * NCORE, LANES))
     meta = lax.all_to_all(meta, ("z", "x", "core"), 0, 0).reshape(NZ, NX * NCORE, LANES)
-
-    start = rep * ROWS + jnp.minimum(meta[0, 0, 0] + 2, 0)
-    a_all = lax.dynamic_slice_in_dim(a_blocks, start, ROWS, 0).reshape(PAIR, BS, BS)
-    a_all = lax.all_gather(a_all, COL)
 
     def send(lo, size):
         outs = pack(meta, own, other, b_own, b_low, b_high, lo, size)

time: 131 us -> 119 us (0.908)
  waiting for transfers between devices: 61.2 us -> 52.5 us
  starting transfers between devices: 32.7 us -> 26.9 us
  local copies, waits for them, and re-layouts: 4.31 us -> 7.8 us
    ppermute x3, waiting for transfers between devices: 11.8 us -> 4.01 us  [shift_y(): lax.ppermute(value, ('yl', 'rep'), [(y_index(y), y_index((y + steps) % n)...]
    ppermute x7, starting transfers between devices: 16.8 us -> 10.5 us  [shift_z(): return lax.ppermute(value, 'z', [(z, (z + steps) % NZ) for z in range(NZ)])]
    all_to_all x1, waiting for transfers between devices: 9.25 us -> 3.11 us  [body(): lax.all_to_all(meta, ('z', 'x', 'core'), 0, 0)]
    ppermute x7, waiting for transfers between devices: 40.1 us -> 45.3 us  [shift_z(): return lax.ppermute(value, 'z', [(z, (z + steps) % NZ) for z in range(NZ)])]
    unnamed x24, local copies, waits for them, and re-layouts: 0.05 us -> 3 us
  transfers between devices with their start and end apart: 12 -> 12, of which waited for: 7 -> 6; matrix products, arithmetic and copies ran while one was open for 2% -> 5% of each run, Pallas kernels for 7% -> 8%
where the time goes in v3:
time: 119 us
  waiting for transfers between devices  52.5 us (44%)
  starting transfers between devices  26.9 us (23%)
  between operations  14.9 us (13%)
  Pallas kernels  13.8 us (12%)
  local copies, waits for them, and re-layouts  7.8 us (7%)
  other arithmetic  2.79 us (2%)
    ppermute x7, waiting for transfers between devices, shift_z(): return lax.ppermute(value, 'z', [(z, (z + steps) % NZ) for z in range(NZ)])  45.3 us
    all_to_all x1, starting transfers between devices, body(): lax.all_to_all(meta, ('z', 'x', 'core'), 0, 0)  12.4 us
    ppermute x7, starting transfers between devices, shift_z(): return lax.ppermute(value, 'z', [(z, (z + steps) % NZ) for z in range(NZ)])  10.5 us
    pallas_call x2, Pallas kernels, consume(): pl.pallas_call(functools.partial(consume_kernel, shifts, parts, final), o...  8.99 us
    pallas_call x1, Pallas kernels, pack(): pl.pallas_call(functools.partial(pack_kernel, lo, size), out_shape=[jax.S...  4.8 us
    ppermute x3, waiting for transfers between devices, shift_y(): lax.ppermute(value, ('yl', 'rep'), [(y_index(y), y_index((y + steps) % n)...  4.01 us
    ppermute x3, starting transfers between devices, shift_y(): lax.ppermute(value, ('yl', 'rep'), [(y_index(y), y_index((y + steps) % n)...  3.87 us
    all_to_all x1, waiting for transfers between devices, body(): lax.all_to_all(meta, ('z', 'x', 'core'), 0, 0)  3.11 us
  transfers between devices with their start and end apart: 12, of which 6 were waited for; matrix products, arithmetic and copies ran while one was open for 5% of the time, Pallas kernels for 8%

profile of v3, /device:TPU:1, one launch (start us, length us, event | category | flops | bytes accessed | tf_op | source)
XLA Modules:
  0.0 118.8 jit_solution(289390510951882650)
XLA Ops:
  6.5 1.2 %copy-done = bf16[8,2,2,128,128]{4,3,2,1,0:T(8,128)(2,1)S(1)} copy-done((bf16[8,2,2,128,128]{4,3,2,1,0:T(8,128)(2,1)S(1)}, bf16[8,2,2,128,128]{4,3,2,1,0:T(8,128)(2,1)}, u32[]{:S(2)}) %copy-start) | copy-done | bytes 1048600
  7.8 0.8 constant_dynamic-slice_fusion
  8.6 0.0 all-gather.2.cloned.1.call-update
  8.6 2.3 %slice_bitcast_fusion = (bf16[16,128,128]{2,1,0:T(8,128)(2,1)}, bf16[16,128,128]{2,1,0:T(8,128)(2,1)}) fusion(bf16[1,1,32,128,128]{4,3,2,1,0:T(8,128)(2,1)} %param.14), kind=kLoop, calls=%fused_computation | loop fusion | bytes 2097152 | tf_op jit(solution)/shard_map/slice | solution.py:199
  11.0 3.6 %collective-permute-start.9 = (bf16[16,128,128]{2,1,0:T(8,128)(2,1)}, bf16[16,128,128]{2,1,0:T(8,128)(2,1)S(1)}, u32[]{:S(2)}, u32[]{:S(2)}) collective-permute-start(bf16[16,128,128]{2,1,0:T(8,128)(2,1)} %get-tuple-element.94), channel_id=1, source_target_pairs={{0,17},{16,0},{1,16},{17,1},{2,19},{18,2},{3,18},{19,3},{4,21},{20... | collective-permute-start | bytes 1572872 | tf_op jit(solution)/shard_map/ppermute | solution.py:30
  14.5 0.0 collective-permute-start.8
  14.5 0.7 compare_select_fusion
  15.2 0.7 fusion
  15.9 0.1 copy.19
  16.0 0.1 reshape.86
  16.1 0.1 copy.18
  16.2 0.1 reshape.85
  16.3 0.1 pad_add_fusion.1
  16.4 0.6 broadcast_in_dim.28
  17.0 12.4 %all-to-all-start = ((s32[64,1,128]{2,1,0:T(1,128)}), s32[64,1,128]{2,1,0:T(1,128)S(1)}, u32[]{:S(2)}, u32[]{:S(2)}) async-start(s32[64,1,128]{2,1,0:T(1,128)} %broadcast_in_dim.28), calls=%async_computation | async-start | bytes 65536 | tf_op jit(solution)/shard_map/all_to_all | solution.py:204
  30.1 0.7 compare_select_fusion.1
  30.7 0.7 pad_add_fusion.own
  31.4 0.3 collective-permute-start.7
  31.7 4.0 %collective-permute-done.7.other = s32[2,32]{1,0:T(2,128)S(1)} collective-permute-done((s32[2,32]{1,0:T(2,128)S(1)}, s32[2,32]{1,0:T(2,128)S(1)}, u32[]{:S(2)}, u32[]{:S(2)}) %collective-permute-start.7) | collective-permute-done | bytes 288 | tf_op jit(solution)/shard_map/ppermute | solution.py:30
  35.7 3.1 %all-to-all-done = s32[64,1,128]{2,1,0:T(1,128)S(1)} async-done(((s32[64,1,128]{2,1,0:T(1,128)}), s32[64,1,128]{2,1,0:T(1,128)S(1)}, u32[]{:S(2)}, u32[]{:S(2)}) %all-to-all-start) | async-done | bytes 32800 | tf_op jit(solution)/shard_map/all_to_all | solution.py:204
  38.8 0.0 collective-permute-done.9.b_high
  38.8 0.0 collective-permute-done.8.b_low
  38.8 0.8 copy-done.3
  39.6 0.2 copy-done.5
  39.8 0.0 copy-done.2
  39.8 4.8 %pack.3 = (bf16[1296,128]{1,0:T(8,128)(2,1)}, bf16[1296,128]{1,0:T(8,128)(2,1)S(1)}, bf16[1296,128]{1,0:T(8,128)(2,1)S(1)}, bf16[1296,128]{1,0:T(8,128)(2,1)S(1)...) custom-call(s32[8,8,128]{2,1,0:T(8,128)S(1)} %bitcast.22, ...), custom_call_target="tpu_custom_call" | custom-call | tf_op jit(solution)/shard_map/pack/pallas_call | solution.py:105
  44.7 2.2 %collective-permute-start.10 = (bf16[1296,128]{1,0:T(8,128)(2,1)S(1)}, bf16[1296,128]{1,0:T(8,128)(2,1)S(1)}, u32[]{:S(2)}, u32[]{:S(2)}) collective-permute-start(bf16[1296,128]{1,0:T(8,128)(2,1)S(1)} %get-tuple-element.81), channel_id=1, source_target_pairs={{0,128},{32,160},{64,192},{96,224},{128,0},{160,32},{192,64},{224,... | collective-permute-start | bytes 995336 | tf_op jit(solution)/shard_map/ppermute | solution.py:36
  46.8 1.2 collective-permute-start.11
  48.0 3.3 %collective-permute-start.12 = (bf16[1296,128]{1,0:T(8,128)(2,1)S(1)}, bf16[1296,128]{1,0:T(8,128)(2,1)}, u32[]{:S(2)}, u32[]{:S(2)}) collective-permute-start(bf16[1296,128]{1,0:T(8,128)(2,1)S(1)} %get-tuple-element.83), channel_id=1, source_target_pairs={{0,160},{32,192},{64,224},{96,0},{128,32},{160,64},{192,96},{224,1... | collective-permute-start | bytes 995336 | tf_op jit(solution)/shard_map/ppermute | solution.py:36
  51.3 0.5 collective-permute-start.13
  51.7 3.1 %collective-permute-start.14 = (bf16[1296,128]{1,0:T(8,128)(2,1)S(1)}, bf16[1296,128]{1,0:T(8,128)(2,1)}, u32[]{:S(2)}, u32[]{:S(2)}) collective-permute-start(bf16[1296,128]{1,0:T(8,128)(2,1)S(1)} %get-tuple-element.87), channel_id=1, source_target_pairs={{0,192},{32,224},{64,0},{96,32},{128,64},{160,96},{192,128},{224,1... | collective-permute-start | bytes 995336 | tf_op jit(solution)/shard_map/ppermute | solution.py:36
  54.9 12.3 %collective-permute-done.10.rest_1_ = bf16[1296,128]{1,0:T(8,128)(2,1)S(1)} collective-permute-done((bf16[1296,128]{1,0:T(8,128)(2,1)S(1)}, bf16[1296,128]{1,0:T(8,128)(2,1)S(1)}, u32[]{:S(2)}, u32[]{:S(2)}) %collective-permute-start.10) | collective-permute-done | bytes 331808 | tf_op jit(solution)/shard_map/ppermute | solution.py:36
  67.2 0.3 collective-permute-start.15
  67.5 19.6 %collective-permute-done.11.rest_2_ = bf16[1296,128]{1,0:T(8,128)(2,1)S(1)} collective-permute-done((bf16[1296,128]{1,0:T(8,128)(2,1)S(1)}, bf16[1296,128]{1,0:T(8,128)(2,1)S(1)}, u32[]{:S(2)}, u32[]{:S(2)}) %collective-permute-start.11) | collective-permute-done | bytes 331808 | tf_op jit(solution)/shard_map/ppermute | solution.py:36
  87.1 0.0 collective-permute-start.16
  87.2 0.0 copy-done.8
  87.2 0.7 copy-done.10
  87.9 0.0 collective-permute-done.12.rest_3_
  87.9 0.1 broadcast_3_total_in.2.total_in
  88.0 4.9 %consume.4 = (f32[16,128,128]{2,1,0:T(8,128)S(1)}, s32[8,128]{1,0:T(8,128)S(1)}) custom-call(bf16[8,16,128,128]{3,2,1,0:T(8,128)(2,1)} %all-gather.2.cloned.1.call-done.a_all, f32[16,128,128]{2,1,0:T(8,128)S(1)} %broadcast_3_total_in.2.total_in, s32[8,128]{1,0:T(8,128)S(1)} %broadcast_in_dim.25.longest_in, bf16[1296,128]{1,0:T(8,128)(2,1)} %get-tuple-element.80.rest_0_, ...), custom_call_target="tpu_custom_call" | custom-call | flops 167772160 | bytes 8388608 | tf_op jit(solution)/shard_map/consume/pallas_call | solution.py:163
  93.0 0.0 collective-permute-done.13.rest_0_
  93.0 6.2 %collective-permute-done.14.rest_1_ = bf16[1296,128]{1,0:T(8,128)(2,1)} collective-permute-done((bf16[1296,128]{1,0:T(8,128)(2,1)S(1)}, bf16[1296,128]{1,0:T(8,128)(2,1)}, u32[]{:S(2)}, u32[]{:S(2)}) %collective-permute-start.14) | collective-permute-done | bytes 331808 | tf_op jit(solution)/shard_map/ppermute | solution.py:36
  99.1 7.2 %collective-permute-done.15.rest_2_ = bf16[1296,128]{1,0:T(8,128)(2,1)} collective-permute-done((bf16[1296,128]{1,0:T(8,128)(2,1)S(1)}, bf16[1296,128]{1,0:T(8,128)(2,1)}, u32[]{:S(2)}, u32[]{:S(2)}) %collective-permute-start.15) | collective-permute-done | bytes 331808 | tf_op jit(solution)/shard_map/ppermute | solution.py:36
  106.4 0.0 collective-permute-done.16.rest_3_
  106.4 0.0 copy-done.1
  106.4 4.1 %consume.5 = (bf16[16,128,128]{2,1,0:T(8,128)(2,1)}, s32[8,128]{1,0:T(8,128)S(1)}) custom-call(bf16[8,16,128,128]{3,2,1,0:T(8,128)(2,1)S(1)} %copy-done.1, f32[16,128,128]{2,1,0:T(8,128)S(1)} %get-tuple-element.84.total_in, s32[8,128]{1,0:T(8,128)S(1)} %get-tuple-element.85.longest_in, bf16[1296,128]{1,0:T(8,128)(2,1)} %collective-permute-done.13.rest_0_, ...), custom_call_target="tpu_custom_call" | custom-call | flops 167772160 | bytes 8388608 | tf_op jit(solution)/shard_map/consume/pallas_call | solution.py:163
  110.5 0.5 slice.19
  111.7 0.2 conditional.1
  (21 shorter events, 0.0 us)
Async XLA Ops:
  6.5 1.2 %copy-start = (bf16[8,2,2,128,128]{4,3,2,1,0:T(8,128)(2,1)S(1)}, bf16[8,2,2,128,128]{4,3,2,1,0:T(8,128)(2,1)}, u32[]{:S(2)}) copy-start(bf16[8,2,2,128,128]{4,3,2,1,0:T(8,128)(2,1)} %param.11) | copy-start | bytes 3145732
  6.5 33.3 %copy-start.2 = (bf16[1,1,32,128,128]{4,3,2,1,0:T(8,128)(2,1)S(1)}, bf16[1,1,32,128,128]{4,3,2,1,0:T(8,128)(2,1)}, u32[]{:S(2)}) copy-start(bf16[1,1,32,128,128]{4,3,2,1,0:T(8,128)(2,1)} %param.14) | copy-start | bytes 3145732
  6.5 81.4 %all-gather.2.cloned.1.call-start = ((), (), s32[]{:S(2)}) async-start(), calls=%async_computation.1 | async-start | bytes 4718592 | tf_op jit(solution)/shard_map/all_gather | solution.py:195
  11.0 27.9 %collective-permute-start.9 = (bf16[16,128,128]{2,1,0:T(8,128)(2,1)}, bf16[16,128,128]{2,1,0:T(8,128)(2,1)S(1)}, u32[]{:S(2)}, u32[]{:S(2)}) collective-permute-start(bf16[16,128,128]{2,1,0:T(8,128)(2,1)} %get-tuple-element.94), channel_id=1, source_target_pairs={{0,17},{16,0},{1,16},{17,1},{2,19},{18,2},{3,18},{19,3},{4,21},{20... | collective-permute-start | bytes 1572872 | tf_op jit(solution)/shard_map/ppermute | solution.py:30
  14.5 24.3 %collective-permute-start.8 = (bf16[16,128,128]{2,1,0:T(8,128)(2,1)}, bf16[16,128,128]{2,1,0:T(8,128)(2,1)S(1)}, u32[]{:S(2)}, u32[]{:S(2)}) collective-permute-start(bf16[16,128,128]{2,1,0:T(8,128)(2,1)} %get-tuple-element.95), channel_id=1, source_target_pairs={{0,16},{16,1},{1,17},{17,0},{2,18},{18,3},{3,19},{19,2},{4,20},{20... | collective-permute-start | bytes 1572872 | tf_op jit(solution)/shard_map/ppermute | solution.py:30
  17.0 21.8 %all-to-all-start = ((s32[64,1,128]{2,1,0:T(1,128)}), s32[64,1,128]{2,1,0:T(1,128)S(1)}, u32[]{:S(2)}, u32[]{:S(2)}) async-start(s32[64,1,128]{2,1,0:T(1,128)} %broadcast_in_dim.28), calls=%async_computation | async-start | bytes 65536 | tf_op jit(solution)/shard_map/all_to_all | solution.py:204
  31.4 4.3 %collective-permute-start.7 = (s32[2,32]{1,0:T(2,128)S(1)}, s32[2,32]{1,0:T(2,128)S(1)}, u32[]{:S(2)}, u32[]{:S(2)}) collective-permute-start(s32[2,32]{1,0:T(2,128)S(1)} %pad_add_fusion.own), channel_id=1, source_target_pairs={{0,16},{16,1},{1,17},{17,0},{2,18},{18,3},{3,19},{19,2},{4,20},{20... | collective-permute-start | bytes 776 | tf_op jit(solution)/shard_map/ppermute | solution.py:30
  38.8 0.8 copy-start.3
  38.8 1.0 copy-start.5
  44.7 22.5 %collective-permute-start.10 = (bf16[1296,128]{1,0:T(8,128)(2,1)S(1)}, bf16[1296,128]{1,0:T(8,128)(2,1)S(1)}, u32[]{:S(2)}, u32[]{:S(2)}) collective-permute-start(bf16[1296,128]{1,0:T(8,128)(2,1)S(1)} %get-tuple-element.81), channel_id=1, source_target_pairs={{0,128},{32,160},{64,192},{96,224},{128,0},{160,32},{192,64},{224,... | collective-permute-start | bytes 995336 | tf_op jit(solution)/shard_map/ppermute | solution.py:36
  46.8 40.3 %collective-permute-start.11 = (bf16[1296,128]{1,0:T(8,128)(2,1)S(1)}, bf16[1296,128]{1,0:T(8,128)(2,1)S(1)}, u32[]{:S(2)}, u32[]{:S(2)}) collective-permute-start(bf16[1296,128]{1,0:T(8,128)(2,1)S(1)} %get-tuple-element.82), channel_id=1, source_target_pairs={{0,96},{32,128},{64,160},{96,192},{128,224},{160,0},{192,32},{224,... | collective-permute-start | bytes 995336 | tf_op jit(solution)/shard_map/ppermute | solution.py:36
  48.0 39.9 %collective-permute-start.12 = (bf16[1296,128]{1,0:T(8,128)(2,1)S(1)}, bf16[1296,128]{1,0:T(8,128)(2,1)}, u32[]{:S(2)}, u32[]{:S(2)}) collective-permute-start(bf16[1296,128]{1,0:T(8,128)(2,1)S(1)} %get-tuple-element.83), channel_id=1, source_target_pairs={{0,160},{32,192},{64,224},{96,0},{128,32},{160,64},{192,96},{224,1... | collective-permute-start | bytes 995336 | tf_op jit(solution)/shard_map/ppermute | solution.py:36
  51.3 41.7 %collective-permute-start.13 = (bf16[1296,128]{1,0:T(8,128)(2,1)S(1)}, bf16[1296,128]{1,0:T(8,128)(2,1)}, u32[]{:S(2)}, u32[]{:S(2)}) collective-permute-start(bf16[1296,128]{1,0:T(8,128)(2,1)S(1)} %get-tuple-element.86), channel_id=1, source_target_pairs={{0,64},{32,96},{64,128},{96,160},{128,192},{160,224},{192,0},{224,... | collective-permute-start | bytes 995336 | tf_op jit(solution)/shard_map/ppermute | solution.py:36
  51.7 47.4 %collective-permute-start.14 = (bf16[1296,128]{1,0:T(8,128)(2,1)S(1)}, bf16[1296,128]{1,0:T(8,128)(2,1)}, u32[]{:S(2)}, u32[]{:S(2)}) collective-permute-start(bf16[1296,128]{1,0:T(8,128)(2,1)S(1)} %get-tuple-element.87), channel_id=1, source_target_pairs={{0,192},{32,224},{64,0},{96,32},{128,64},{160,96},{192,128},{224,1... | collective-permute-start | bytes 995336 | tf_op jit(solution)/shard_map/ppermute | solution.py:36
  67.2 20.0 %copy-start.8 = (bf16[1296,128]{1,0:T(8,128)(2,1)}, bf16[1296,128]{1,0:T(8,128)(2,1)S(1)}, u32[]{:S(2)}) copy-start(bf16[1296,128]{1,0:T(8,128)(2,1)S(1)} %collective-permute-done.10.rest_1_) | copy-start | bytes 995332
  67.2 39.2 %collective-permute-start.15 = (bf16[1296,128]{1,0:T(8,128)(2,1)S(1)}, bf16[1296,128]{1,0:T(8,128)(2,1)}, u32[]{:S(2)}, u32[]{:S(2)}) collective-permute-start(bf16[1296,128]{1,0:T(8,128)(2,1)S(1)} %get-tuple-element.88), channel_id=1, source_target_pairs={{0,32},{32,64},{64,96},{96,128},{128,160},{160,192},{192,224},{224... | collective-permute-start | bytes 995336 | tf_op jit(solution)/shard_map/ppermute | solution.py:36
  87.1 0.8 copy-start.10
  87.1 19.2 %collective-permute-start.16 = (bf16[1296,128]{1,0:T(8,128)(2,1)S(1)}, bf16[1296,128]{1,0:T(8,128)(2,1)}, u32[]{:S(2)}, u32[]{:S(2)}) collective-permute-start(bf16[1296,128]{1,0:T(8,128)(2,1)S(1)} %get-tuple-element.89), channel_id=1, source_target_pairs={{0,224},{32,0},{64,32},{96,64},{128,96},{160,128},{192,160},{224,1... | collective-permute-start | bytes 995336 | tf_op jit(solution)/shard_map/ppermute | solution.py:36
  87.9 18.5 %copy-start.1 = (bf16[8,16,128,128]{3,2,1,0:T(8,128)(2,1)S(1)}, bf16[8,16,128,128]{3,2,1,0:T(8,128)(2,1)}, u32[]{:S(2)}) copy-start(bf16[8,16,128,128]{3,2,1,0:T(8,128)(2,1)} %all-gather.2.cloned.1.call-done.a_all) | copy-start | bytes 12582916
  92.9 18.8 %copy-start.4 = (bf16[16,128,128]{2,1,0:T(8,128)(2,1)S(1)}, bf16[16,128,128]{2,1,0:T(8,128)(2,1)}, u32[]{:S(2)}) copy-start(bf16[16,128,128]{2,1,0:T(8,128)(2,1)} %copy-done.3) | copy-start | bytes 1572868
  92.9 18.8 %copy-start.6 = (bf16[16,128,128]{2,1,0:T(8,128)(2,1)S(1)}, bf16[16,128,128]{2,1,0:T(8,128)(2,1)}, u32[]{:S(2)}) copy-start(bf16[16,128,128]{2,1,0:T(8,128)(2,1)} %copy-done.5) | copy-start | bytes 1572868
  92.9 18.8 %copy-start.7 = (bf16[1296,128]{1,0:T(8,128)(2,1)S(1)}, bf16[1296,128]{1,0:T(8,128)(2,1)}, u32[]{:S(2)}) copy-start(bf16[1296,128]{1,0:T(8,128)(2,1)} %get-tuple-element.80.rest_0_) | copy-start | bytes 995332
  92.9 18.8 %copy-start.9 = (bf16[1296,128]{1,0:T(8,128)(2,1)S(1)}, bf16[1296,128]{1,0:T(8,128)(2,1)}, u32[]{:S(2)}) copy-start(bf16[1296,128]{1,0:T(8,128)(2,1)} %copy-done.8) | copy-start | bytes 995332
  93.0 18.8 %copy-start.11 = (bf16[1296,128]{1,0:T(8,128)(2,1)S(1)}, bf16[1296,128]{1,0:T(8,128)(2,1)}, u32[]{:S(2)}) copy-start(bf16[1296,128]{1,0:T(8,128)(2,1)} %copy-done.10) | copy-start | bytes 995332
Sparse Core Ops, SparseCore 0:
  9.2 39.1 all-gather.1
